TPU v7x, 32 devices: a whole 2x2x4 slice. The times are simulated.
32 devices in a mesh: half: 2 (over core), dev: 16 (over z, y, x).
Axes of the slice: x: 2, y: 2, z: 4, core: 2. Of those that a mesh axis runs over, the one named last changes fastest.
Arguments:
- field_mix: float32 [32, 32], P('half'), may hold values from -1 to 1
- alm: bfloat16 [128, 2, 32, 2048], P('dev', None, 'half'), may hold values from -6 to 6
- legendre: bfloat16 [128, 2048, 16], P('dev'), may hold values from -0.125 to 0.125
- order_ids: int32 [128], replicated, may hold values from 0 to 127, each once
- fetch_list: int32 [16, 16, 2], replicated, may hold values from -1 to 31, as said below
- scan_tiles: int32 [64, 32], P('dev'), may hold values from 0 to 31, as said below
- block_tile: int32 [64, 32], P('dev'), may hold values from 0 to 31
- block_pix: int32 [64, 16384], P('dev'), may hold values from -1 to 127, as said below
- noise_kernel: float32 [64, 512], P('dev'), may hold values from -0.24 to 0.24
- scan_weight: float32 [64], P('dev'), may hold values from 0.1 to 1
Outputs:
- binned: float32 [16, 32, 4096], P('dev', 'half')
Inputs may be any that keep to these rules, and one draw needn't show every extreme that they name: `fetch_list`: entry [d, e, k] is the index, among the 32 tiles of device d, of the tile that device e fetches from d in slot k, or -1 for an empty slot; the live slots of one pair come first and name distinct tiles; every device fills all 2 slots from at least one source. `scan_tiles`: entry [n, i] is a slot source 2 + k whose fetch_list[source, n div 4, k] is not -1. `block_pix`: -1 marks a flagged sample.
All inputs are finite; a program needn't handle non-finite values.
Results may differ from a plain program's by a relative error of at most 0.007.
Values may be sent and summed in bfloat16 or wider, within the bound.
A program may use at most 128 MiB of HBM per device.

v0:
```python
import math

import jax
import jax.numpy as jnp
from jax import lax
from jax.sharding import PartitionSpec as P

NPHI = 4096
TILE = 128
BLK = 512


def toeplitz_rows(band_values, block_len):
    scan_count = band_values.shape[0]
    wrapped = jnp.pad(band_values, ((0, 0), (0, 1)))
    repeated = jnp.tile(wrapped, (1, block_len))
    folded = repeated[:, : block_len * (2 * block_len - 1)].reshape(
        scan_count, block_len, 2 * block_len - 1
    )
    return folded[:, :, block_len - 1 :]


def local(
    field_mix,
    alm,
    legendre,
    order_ids,
    fetch_list,
    scan_tiles,
    block_tile,
    block_pix,
    noise_kernel,
    scan_weight,
):
    highest = lax.Precision.HIGHEST
    device_count = lax.axis_size("dev")
    position = lax.axis_index("dev")
    both_halves = lax.all_gather(alm, "half", axis=2, tiled=True)
    mixed_alm = jnp.einsum(
        "fg,scgl->scfl", field_mix, both_halves.astype(jnp.float32), precision=highest
    ).astype(jnp.bfloat16)
    cycle_coeff = jnp.einsum(
        "scfl,slr->rscf", mixed_alm, legendre, preferred_element_type=jnp.float32
    ).astype(jnp.bfloat16)
    by_cycle = lax.all_to_all(cycle_coeff, "dev", split_axis=0, concat_axis=1, tiled=True)
    cycle_count = by_cycle.shape[0]
    order_count = by_cycle.shape[1]
    field_count = by_cycle.shape[3]
    pixel_block = 512
    block_count = NPHI // pixel_block
    weights = jnp.where(order_ids == 0, 1.0, 2.0).astype(jnp.float32) / math.sqrt(2.0 * order_count)

    def cycle_block(start):
        pixel_iota = start + jnp.arange(pixel_block, dtype=jnp.int32)
        phase_steps = order_ids[:, None] * (2 * pixel_iota[None, :] + 1) % (2 * NPHI)
        angles = phase_steps.astype(jnp.float32) * (math.pi / NPHI)
        fourier = jnp.stack(
            [weights[:, None] * jnp.cos(angles), -weights[:, None] * jnp.sin(angles)], axis=1
        ).astype(jnp.bfloat16)
        return jnp.einsum(
            "rscf,scj->rfj", by_cycle, fourier, preferred_element_type=jnp.float32
        ).astype(jnp.bfloat16)

    starts = jnp.arange(block_count, dtype=jnp.int32) * pixel_block
    cycle_blocks = lax.map(cycle_block, starts)
    per_block = pixel_block // TILE
    map_tiles = cycle_blocks.reshape(block_count, cycle_count, field_count, per_block, TILE)
    map_tiles = map_tiles.transpose(1, 0, 3, 2, 4).reshape(
        cycle_count * block_count * per_block, field_count, TILE
    )
    tile_count = map_tiles.shape[0]
    slot_capacity = fetch_list.shape[2]
    owner_row = lax.dynamic_index_in_dim(fetch_list, position, 0, keepdims=False)
    outgoing = (
        map_tiles[jnp.maximum(owner_row, 0)]
        * (owner_row >= 0).astype(jnp.bfloat16)[:, :, None, None]
    )
    fetched = lax.all_to_all(outgoing, "dev", split_axis=0, concat_axis=0, tiled=True)
    slot_total = device_count * slot_capacity
    flat_fetched = fetched.reshape(slot_total, field_count, TILE)
    scan_count = block_tile.shape[0]
    block_total = block_tile.shape[1]
    slot_index = jnp.take_along_axis(scan_tiles, block_tile, axis=1)
    block_tiles = flat_fetched[slot_index]
    pixels = block_pix.reshape(scan_count, block_total, BLK)
    one_hot = (
        pixels[:, :, None, :] == jnp.arange(TILE, dtype=jnp.int32)[None, None, :, None]
    ).astype(jnp.bfloat16)
    samples = jnp.einsum(
        "sbfp,sbpt->sbft", block_tiles, one_hot, preferred_element_type=jnp.float32
    ).astype(jnp.bfloat16)
    taps = noise_kernel.astype(jnp.bfloat16)
    near_band = jnp.concatenate([taps[:, ::-1], taps[:, 1:]], axis=1)
    far_band = jnp.concatenate(
        [jnp.zeros((scan_count, BLK), jnp.bfloat16), taps[:, 1:][:, ::-1]], axis=1
    )
    near_table = toeplitz_rows(near_band, BLK)
    far_table = toeplitz_rows(far_band, BLK)
    earlier = jnp.pad(samples[:, :-1], ((0, 0), (1, 0), (0, 0), (0, 0)))
    later = jnp.pad(samples[:, 1:], ((0, 0), (0, 1), (0, 0), (0, 0)))
    filtered = jnp.einsum("sbfu,stu->sbft", samples, near_table, preferred_element_type=jnp.float32)
    filtered = filtered + jnp.einsum(
        "sbfu,stu->sbft", earlier, far_table, preferred_element_type=jnp.float32
    )
    filtered = filtered + jnp.einsum(
        "sbfu,sut->sbft", later, far_table, preferred_element_type=jnp.float32
    )
    weighted = (scan_weight[:, None, None, None] * filtered).astype(jnp.bfloat16)
    partial_value = jnp.einsum(
        "sbft,sbpt->sbfp", weighted, one_hot, preferred_element_type=jnp.float32
    )
    flat_slots = slot_index.reshape(-1)
    slot_select = (jnp.arange(slot_total, dtype=jnp.int32)[:, None] == flat_slots[None, :]).astype(
        jnp.float32
    )
    per_slot = jnp.dot(
        slot_select,
        partial_value.reshape(scan_count * block_total, field_count * TILE),
        precision=highest,
    )
    per_slot = per_slot.reshape(device_count, slot_capacity, field_count, TILE)
    returned = lax.all_to_all(per_slot, "dev", split_axis=0, concat_axis=0, tiled=True)
    owner_select = (
        jnp.arange(tile_count, dtype=jnp.int32)[:, None] == owner_row.reshape(-1)[None, :]
    ).astype(jnp.float32)
    own_tiles = jnp.dot(
        owner_select, returned.reshape(slot_total, field_count * TILE), precision=highest
    )
    binned = own_tiles.reshape(cycle_count, NPHI // TILE, field_count, TILE).transpose(0, 2, 1, 3)
    return binned.reshape(cycle_count, field_count, NPHI)


def solution(mesh):
    return jax.shard_map(
        local,
        mesh=mesh,
        in_specs=(
            P("half", None),
            P("dev", None, "half", None),
            P("dev", None, None),
            P(),
            P(),
            P("dev", None),
            P("dev", None),
            P("dev", None),
            P("dev", None),
            P("dev"),
        ),
        out_specs=P("dev", "half", None),
        check_vma=False,
    )
```

profile of v0, /device:TPU:0, one launch (start us, length us, event | category | flops | bytes accessed | tf_op | source)
XLA Modules:
  0.0 158.0 jit_solution(2847369865432307556)
XLA Ops:
  6.5 0.7 all-gather.2.cloned.1.call-update
  7.3 0.7 convert_element_type.83
  8.0 0.4 rev.6
  8.4 0.4 reverse
  8.8 0.7 fusion.38
  9.8 0.7 negate_bitcast_fusion
  10.4 0.7 bitcast_or_fusion
  11.1 2.5 %broadcast_bitcast_fusion.1 = bf16[1,4,512,1024]{3,2,1,0:T(8,128)(2,1)} fusion(bf16[4,1024]{1,0:T(4,128)(2,1)S(1)} %fusion.32), kind=kLoop, calls=%fused_computation.35 | loop fusion | bytes 4202496
  13.7 2.5 %broadcast_bitcast_fusion = bf16[1,4,512,1024]{3,2,1,0:T(8,128)(2,1)} fusion(bf16[4,1024]{1,0:T(4,128)(2,1)S(1)} %pad.28), kind=kLoop, calls=%fused_computation.34 | loop fusion | bytes 4202496
  16.1 6.1 %all-gather.2.cloned.1.call-done = bf16[8,2,32,2048]{3,2,1,0:T(8,128)(2,1)} async-done(((bf16[8,2,16,2048]{3,2,1,0:T(8,128)(2,1)}), bf16[8,2,32,2048]{3,2,1,0:T(8,128)(2,1)}) %all-gather.2.cloned.1.call-update) | async-done | bytes 2097168 | tf_op jit(solution)/shard_map/all_gather | solution.py:38
  22.2 2.8 %fusion.15 = bf16[8,2,16,2048]{3,2,1,0:T(8,128)(2,1)S(1)} fusion(bf16[8,2,32,2048]{3,2,1,0:T(8,128)(2,1)} %all-gather.2.cloned.1.call-done, f32[16,32]{1,0:T(8,128)S(1)} %copy-done.6), kind=kOutput, calls=%fused_computation.30 | convolution fusion | flops 201850880 | bytes 3147776 | tf_op jit(solution)/shard_map/fg,scgl->scfl/dot_general | solution.py:39
  25.0 0.4 fusion.21
  25.6 0.7 reshape.413
  26.3 6.8 %all-to-all-start = ((bf16[16,2,128]{2,1,0:T(2,128)(2,1)}), bf16[16,2,128]{2,1,0:T(2,128)(2,1)S(1)}, u32[]{:S(2)}, u32[]{:S(2)}) async-start(bf16[16,2,128]{2,1,0:T(2,128)(2,1)} %reshape.413), calls=%async_computation | async-start | bytes 16384 | tf_op jit(solution)/shard_map/all_to_all | solution.py:45
  33.2 1.5 gather_fusion.2
  34.9 5.4 %all-to-all-done = bf16[16,2,128]{2,1,0:T(2,128)(2,1)S(1)} async-done(((bf16[16,2,128]{2,1,0:T(2,128)(2,1)}), bf16[16,2,128]{2,1,0:T(2,128)(2,1)S(1)}, u32[]{:S(2)}, u32[]{:S(2)}) %all-to-all-start) | async-done | bytes 8224 | tf_op jit(solution)/shard_map/all_to_all | solution.py:45
  40.4 21.5 %while.12 = (s32[]{:T(128)}, bf16[8,1,16,512]{3,2,1,0:T(8,128)(2,1)S(1)}, f32[128]{0:T(128)S(1)}, s32[128]{0:T(128)S(1)}, s32[8]{0:T(128)S(1)}, /*index=5*/f32[1...) while((s32[]{:T(128)}, bf16[8,1,16,512]{3,2,1,0:T(8,128)(2,1)S(1)}, f32[128]{0:T(128)S(1)}, ...), condition=%wide.region_1.2_spmd, body=%wide.region_0.1_spmd.sunk | while | flops 5514754 | bytes 554609 | solution.py:65
  40.4 0.6 dynamic_slice.15
  41.0 0.6 multiply_add_fusion.3
  41.7 1.3 multiply_convert_fusion.4
  43.1 0.6 dynamic_slice.15
  43.7 0.6 multiply_add_fusion.3
  44.4 1.3 multiply_convert_fusion.4
  45.8 0.6 dynamic_slice.15
  46.4 0.6 multiply_add_fusion.3
  47.1 1.3 multiply_convert_fusion.4
  48.5 0.6 dynamic_slice.15
  49.1 0.6 multiply_add_fusion.3
  49.7 1.3 multiply_convert_fusion.4
  51.2 0.6 dynamic_slice.15
  51.8 0.6 multiply_add_fusion.3
  52.4 1.3 multiply_convert_fusion.4
  53.9 0.6 dynamic_slice.15
  54.4 0.6 multiply_add_fusion.3
  55.1 1.3 multiply_convert_fusion.4
  56.5 0.6 dynamic_slice.15
  57.1 0.6 multiply_add_fusion.3
  57.8 1.3 multiply_convert_fusion.4
  59.2 0.6 dynamic_slice.15
  59.8 0.6 multiply_add_fusion.3
  60.5 1.3 multiply_convert_fusion.4
  62.0 0.6 gather_fusion
  62.6 0.8 broadcast_multiply_fusion
  63.3 3.7 %all-to-all-start.1 = ((bf16[16,2,16,128]{3,2,1,0:T(8,128)(2,1)}), bf16[16,2,16,128]{3,2,1,0:T(8,128)(2,1)S(1)}, u32[]{:S(2)}, u32[]{:S(2)}) async-start(bf16[16,2,16,128]{3,2,1,0:T(8,128)(2,1)} %broadcast_multiply_fusion), calls=%async_computation.1 | async-start | bytes 262144 | tf_op jit(solution)/shard_map/all_to_all | solution.py:78
  67.3 5.4 %copy.51 = bf16[1,4,512,1024]{3,1,2,0:T(4,128)(2,1)S(1)} copy(bf16[1,4,512,1024]{3,2,1,0:T(8,128)(2,1)} %broadcast_bitcast_fusion.1) | data formatting | bytes 8388608
  72.7 3.2 %slice.36 = bf16[4,523776]{1,0:T(4,128)(2,1)} slice(bf16[4,524288]{1,0:T(4,128)(2,1)S(1)} %bitcast.128), slice={[0:4], [0:523776]} | slice | bytes 8380416 | tf_op jit(solution)/shard_map/slice | solution.py:17
  75.9 5.7 %reshape.409 = bf16[2095104]{0:T(1024)(128)(2,1)} reshape(bf16[4,523776]{1,0:T(4,128)(2,1)} %slice.36) | data formatting | bytes 8380416
  81.6 10.1 %reshape.364 = bf16[4,512,1023]{2,1,0:T(8,128)(2,1)} reshape(bf16[2095104]{0:T(1024)(128)(2,1)} %reshape.409) | data formatting | bytes 8380416 | tf_op jit(solution)/shard_map/reshape | solution.py:17
  91.7 5.4 %copy.52 = bf16[1,4,512,1024]{3,1,2,0:T(4,128)(2,1)S(1)} copy(bf16[1,4,512,1024]{3,2,1,0:T(8,128)(2,1)} %broadcast_bitcast_fusion) | data formatting | bytes 8388608
  97.2 3.3 %slice.39 = bf16[4,523776]{1,0:T(4,128)(2,1)} slice(bf16[4,524288]{1,0:T(4,128)(2,1)S(1)} %bitcast.129), slice={[0:4], [0:523776]} | slice | bytes 8380416 | tf_op jit(solution)/shard_map/slice | solution.py:17
  100.5 5.7 %reshape.411 = bf16[2095104]{0:T(1024)(128)(2,1)} reshape(bf16[4,523776]{1,0:T(4,128)(2,1)} %slice.39) | data formatting | bytes 8380416
  106.2 10.1 %reshape.365 = bf16[4,512,1023]{2,1,0:T(8,128)(2,1)} reshape(bf16[2095104]{0:T(1024)(128)(2,1)} %reshape.411) | data formatting | bytes 8380416 | tf_op jit(solution)/shard_map/reshape | solution.py:17
  116.3 0.7 gather_fusion.1
  117.0 5.4 %fusion.20 = bf16[4,32,16,512]{3,2,1,0:T(8,128)(2,1)S(1)} fusion(bf16[4,32,16,128]{3,2,1,0:T(8,128)(2,1)S(1)} %bitcast.135, s32[4,32,512]{2,1,0:T(8,128)S(1)} %bitcast.141), kind=kOutput, calls=%fused_computation.39 | convolution fusion | flops 277872640 | bytes 2883584 | tf_op jit(solution)/shard_map/sbfp,sbpt->sbft/dot_general | solution.py:89
  122.4 1.4 fusion.16
  123.8 0.8 copy-done.2
  124.6 1.4 fusion.18
  126.0 1.7 %multiply_convert_fusion.2 = bf16[4,32,16,512]{3,2,1,0:T(8,128)(2,1)S(1)} fusion(f32[4,32,16,512]{3,2,1,0:T(8,128)S(1)} %fusion.16, f32[4,32,16,512]{3,2,1,0:T(8,128)S(1)} %fusion.18, f32[4]{0:T(128)S(1)} %copy-done.8, bf16[4,32,16,512]{3,2,1,0:T(8,128)(2,1)S(1)} %fusion.20, bf16[4,512,1023]{2,1,0:T(8,128)(2,1)S(1)} %copy-done.2), kind=kOutput, calls=%fused_computation.28 | convolution fusion | flops 1044381696 | bytes 14615040 | tf_op jit(solution)/shard_map/sbfu,sut->sbft/dot_general | solution.py:105
  127.7 5.0 %fusion.11 = f32[4,32,16,128]{3,2,1,0:T(8,128)S(1)} fusion(bf16[4,32,16,512]{3,2,1,0:T(8,128)(2,1)S(1)} %multiply_convert_fusion.2, s32[4,32,512]{2,1,0:T(8,128)S(1)} %bitcast.142), kind=kOutput, calls=%fused_computation.24 | convolution fusion | flops 276824064 | bytes 3407872 | tf_op jit(solution)/shard_map/sbft,sbpt->sbfp/dot_general | solution.py:109
  133.4 0.7 fusion.29
  134.1 0.8 copy.40
  134.9 6.7 %all-to-all-start.2 = ((f32[16,2,16,128]{3,2,1,0:T(8,128)}), f32[16,2,16,128]{3,2,1,0:T(8,128)S(1)}, u32[]{:S(2)}, u32[]{:S(2)}) async-start(f32[16,2,16,128]{3,2,1,0:T(8,128)} %copy.40), calls=%async_computation.2 | async-start | bytes 524288 | tf_op jit(solution)/shard_map/all_to_all | solution.py:122
  141.8 8.3 %all-to-all-done.2 = f32[16,2,16,128]{3,2,1,0:T(8,128)S(1)} async-done(((f32[16,2,16,128]{3,2,1,0:T(8,128)}), f32[16,2,16,128]{3,2,1,0:T(8,128)S(1)}, u32[]{:S(2)}, u32[]{:S(2)}) %all-to-all-start.2) | async-done | bytes 262176 | tf_op jit(solution)/shard_map/all_to_all | solution.py:122
  150.4 0.8 reshape.368
  (56 shorter events, 3.7 us)
Async XLA Ops:
  6.5 18.5 %copy-start = (bf16[8,2048,16]{1,2,0:T(8,128)(2,1)S(1)}, bf16[8,2048,16]{1,2,0:T(8,128)(2,1)}, u32[]{:S(2)}) copy-start(bf16[8,2048,16]{1,2,0:T(8,128)(2,1)} %param.14) | copy-start | bytes 1572868
  6.5 15.7 %all-gather.2.cloned.1.call-start = ((), (), s32[]{:S(2)}) async-start(), calls=%async_computation.3 | async-start | bytes 3145728 | tf_op jit(solution)/shard_map/all_gather | solution.py:38
  11.1 11.1 %copy-start.6 = (f32[16,32]{1,0:T(8,128)S(1)}, f32[16,32]{1,0:T(8,128)}, u32[]{:S(2)}) copy-start(f32[16,32]{1,0:T(8,128)} %param.12) | copy-start | bytes 6148
  13.7 19.5 %copy-start.1 = (s32[4,32]{1,0:T(4,128)S(1)}, s32[4,32]{1,0:T(4,128)}, u32[]{:S(2)}) copy-start(s32[4,32]{1,0:T(4,128)} %param.17) | copy-start | bytes 1540
  16.1 24.3 %copy-start.5 = (s32[128]{0:T(128)S(1)}, s32[128]{0:T(128)}, u32[]{:S(2)}) copy-start(s32[128]{0:T(128)} %param.15) | copy-start | bytes 1540
  25.0 42.0 %copy-start.7 = (s32[4,32]{1,0:T(4,128)S(1)}, s32[4,32]{1,0:T(4,128)}, u32[]{:S(2)}) copy-start(s32[4,32]{1,0:T(4,128)} %param.18) | copy-start | bytes 1540
  25.0 42.2 %copy-start.4 = (s32[4,16384]{1,0:T(4,128)S(1)}, s32[4,16384]{1,0:T(4,128)}, u32[]{:S(2)}) copy-start(s32[4,16384]{1,0:T(4,128)} %param.19) | copy-start | bytes 786436
  26.3 14.0 %all-to-all-start = ((bf16[16,2,128]{2,1,0:T(2,128)(2,1)}), bf16[16,2,128]{2,1,0:T(2,128)(2,1)S(1)}, u32[]{:S(2)}, u32[]{:S(2)}) async-start(bf16[16,2,128]{2,1,0:T(2,128)(2,1)} %reshape.413), calls=%async_computation | async-start | bytes 16384 | tf_op jit(solution)/shard_map/all_to_all | solution.py:45
  63.3 52.9 %all-to-all-start.1 = ((bf16[16,2,16,128]{3,2,1,0:T(8,128)(2,1)}), bf16[16,2,16,128]{3,2,1,0:T(8,128)(2,1)S(1)}, u32[]{:S(2)}, u32[]{:S(2)}) async-start(bf16[16,2,16,128]{3,2,1,0:T(8,128)(2,1)} %broadcast_multiply_fusion), calls=%async_computation.1 | async-start | bytes 262144 | tf_op jit(solution)/shard_map/all_to_all | solution.py:78
  117.0 5.4 %copy-start.3 = (bf16[4,512,1023]{2,1,0:T(8,128)(2,1)S(1)}, bf16[4,512,1023]{2,1,0:T(8,128)(2,1)}, u32[]{:S(2)}) copy-start(bf16[4,512,1023]{2,1,0:T(8,128)(2,1)} %reshape.364) | copy-start | bytes 12570628
  122.4 2.2 %copy-start.2 = (bf16[4,512,1023]{2,1,0:T(8,128)(2,1)S(1)}, bf16[4,512,1023]{2,1,0:T(8,128)(2,1)}, u32[]{:S(2)}) copy-start(bf16[4,512,1023]{2,1,0:T(8,128)(2,1)} %reshape.365) | copy-start | bytes 12570628
  124.6 1.4 copy-start.8
  134.9 15.2 %all-to-all-start.2 = ((f32[16,2,16,128]{3,2,1,0:T(8,128)}), f32[16,2,16,128]{3,2,1,0:T(8,128)S(1)}, u32[]{:S(2)}, u32[]{:S(2)}) async-start(f32[16,2,16,128]{3,2,1,0:T(8,128)} %copy.40), calls=%async_computation.2 | async-start | bytes 524288 | tf_op jit(solution)/shard_map/all_to_all | solution.py:122
Sparse Core Ops, SparseCore 0:
  8.9 13.2 all-gather.1
where the time goes:
time: 159 us; the launch traced here: 158 us
  local copies, waits for them, and re-layouts  67.3 us (42%)
  waiting for transfers between devices  20.5 us (13%)
  matrix products  20.3 us (13%)
  other arithmetic  18.9 us (12%)
  starting transfers between devices  17.2 us (11%)
  between operations  13.7 us (9%)
    unnamed x30, local copies, waits for them, and re-layouts  29.8 us
    reshape x2, local copies, waits for them, and re-layouts, toeplitz_rows(): repeated[:, :block_len * (2 * block_len - 1)]  20.2 us
    another operation x8, other arithmetic  10.2 us
    all_to_all x1, waiting for transfers between devices, local(): lax.all_to_all(per_slot, 'dev', split_axis=0, concat_axis=0, tiled=True)  8.33 us
    all_to_all x1, starting transfers between devices, local(): lax.all_to_all(cycle_coeff, 'dev', split_axis=0, concat_axis=1, tiled=True)  6.78 us
    all_to_all x1, starting transfers between devices, local(): lax.all_to_all(per_slot, 'dev', split_axis=0, concat_axis=0, tiled=True)  6.69 us
    slice x2, local copies, waits for them, and re-layouts, toeplitz_rows(): repeated[:, :block_len * (2 * block_len - 1)]  6.47 us
    all_gather x1, waiting for transfers between devices, local(): both_halves = lax.all_gather(alm, 'half', axis=2, tiled=True)  6.09 us
  transfers between devices with their start and end apart: 4, of which 3 were waited for; matrix products, arithmetic and copies ran while one was open for 38% of the time, Pallas kernels for 0%

commit v1 on v0

v1 whole, which is shorter than its diff:
```python
import functools
import math

import jax
import jax.numpy as jnp
from jax import lax
from jax.experimental import pallas as pl
from jax.experimental.pallas import tpu as pltpu
from jax.sharding import PartitionSpec as P

NPHI = 4096
TILE = 128
COLS = 256
VMEM = pltpu.VMEM
SMEM = pltpu.SMEM


def scan_kernel(
    scan_tiles, block_tile, scan_weight, tiles, pix, noise, out, table, padded
):
    scan_count, block_total = block_tile.shape
    length = pix.shape[1]
    block_len = length // block_total
    lags = noise.shape[1]
    fields = tiles.shape[1]
    per_block = block_len // COLS
    halo = lags // COLS
    window = 2 * lags + COLS
    rows = (length // COLS) * fields
    chunk_blocks = 8
    while block_total % chunk_blocks:
        chunk_blocks //= 2
    chunk_rows = chunk_blocks * per_block * fields

    out[...] = jnp.zeros(out.shape, out.dtype)
    padded[pl.ds(0, halo * fields), :] = jnp.zeros((halo * fields, COLS), padded.dtype)
    padded[pl.ds(halo * fields + rows, halo * fields), :] = jnp.zeros(
        (halo * fields, COLS), padded.dtype
    )
    taps = noise[...].astype(jnp.bfloat16).astype(jnp.float32)
    lane = lax.broadcasted_iota(jnp.int32, taps.shape, 1)
    moved = jnp.where(lane == lags - 1, 0.0, pltpu.roll(taps, lags - 1, 1))
    turn = (
        lax.broadcasted_iota(jnp.int32, (TILE, TILE), 0)
        + lax.broadcasted_iota(jnp.int32, (TILE, TILE), 1)
        == TILE - 1
    ).astype(jnp.float32).astype(jnp.bfloat16)
    chunks = lags // TILE
    blank = jnp.zeros((scan_count, TILE), jnp.float32)
    turned = [
        jnp.dot(
            moved[:, c * TILE : (c + 1) * TILE].astype(jnp.bfloat16),
            turn,
            preferred_element_type=jnp.float32,
        )
        for c in range(chunks)
    ]
    band = jnp.concatenate([blank] + turned[::-1] + [taps] + [blank] * 2, axis=1)
    width = band.shape[1]
    top = width - COLS
    for n in range(scan_count):
        strip = pltpu.roll(
            jnp.broadcast_to(band[n : n + 1], (TILE, width)), 0, 1, stride=1, stride_axis=0
        ).astype(jnp.bfloat16)
        for q in range(window // TILE):
            start = top - q * TILE
            table[n, q * TILE : (q + 1) * TILE, :] = strip[:, start : start + COLS]

    def one_scan(n):
        def sample(b, carry):
            slot = scan_tiles[n, block_tile[n, b]]
            tile = tiles[slot].astype(jnp.float32)
            for c in range(block_len // TILE):
                at = pl.multiple_of(b * block_len + c * TILE, TILE)
                index = jnp.broadcast_to(pix[n : n + 1, pl.ds(at, TILE)], tile.shape)
                value = jnp.take_along_axis(
                    tile, jnp.maximum(index, 0), axis=1, mode="promise_in_bounds"
                )
                value = jnp.where(index >= 0, value, 0.0).astype(padded.dtype)
                row = pl.multiple_of((b * per_block + (c * TILE) // COLS + halo) * fields, 16)
                lane_at = (c * TILE) % COLS
                padded[pl.ds(row, fields), lane_at : lane_at + TILE] = value
            return carry

        lax.fori_loop(0, block_total, sample, 0, unroll=4)
        weight = scan_weight[n]

        def chunk(m, carry):
            base = m * chunk_rows
            pieces = [
                padded[pl.ds(pl.multiple_of(base + o * fields, 16), chunk_rows), :]
                for o in range(2 * halo + 1)
            ]
            filtered = jnp.dot(
                jnp.concatenate(pieces, axis=1), table[n], preferred_element_type=jnp.float32
            )
            weighted = (weight * filtered).astype(jnp.bfloat16)
            for k in range(chunk_blocks):
                b = m * chunk_blocks + k
                at = pl.multiple_of(b * block_len, TILE)
                index = pix[n : n + 1, pl.ds(at, block_len)]
                hot = (
                    lax.broadcasted_iota(jnp.int32, (TILE, block_len), 0) == index
                ).astype(jnp.float32).astype(jnp.bfloat16)
                first = k * per_block * fields
                row = jnp.concatenate(
                    [
                        weighted[first + i * fields : first + (i + 1) * fields]
                        for i in range(per_block)
                    ],
                    axis=1,
                )
                part = lax.dot_general(
                    row, hot, (((1,), (1,)), ((), ())), preferred_element_type=jnp.float32
                )
                slot = scan_tiles[n, block_tile[n, b]]
                out[slot] += part
            return carry

        lax.fori_loop(0, block_total // chunk_blocks, chunk, 0)

    for n in range(scan_count):
        one_scan(n)


def scan_part(tiles, scan_tiles, block_tile, block_pix, noise_kernel, scan_weight):
    scan_count, lags = noise_kernel.shape
    fields = tiles.shape[1]
    length = block_pix.shape[1]
    return pl.pallas_call(
        scan_kernel,
        out_shape=jax.ShapeDtypeStruct(tiles.shape, jnp.float32),
        in_specs=[pl.BlockSpec(memory_space=SMEM)] * 3 + [pl.BlockSpec(memory_space=VMEM)] * 3,
        out_specs=pl.BlockSpec(memory_space=VMEM),
        scratch_shapes=[
            VMEM((scan_count, 2 * lags + COLS, COLS), jnp.bfloat16),
            VMEM(((length + 2 * lags) // COLS * fields, COLS), jnp.bfloat16),
        ],
        compiler_params=pltpu.CompilerParams(vmem_limit_bytes=40 * 2**20),
        name="scans",
    )(scan_tiles, block_tile, scan_weight, tiles, block_pix, noise_kernel)


def local(
    field_mix,
    alm,
    legendre,
    order_ids,
    fetch_list,
    scan_tiles,
    block_tile,
    block_pix,
    noise_kernel,
    scan_weight,
):
    highest = lax.Precision.HIGHEST
    device_count = lax.axis_size("dev")
    position = lax.axis_index("dev")
    halves = lax.axis_size("half")
    own = jnp.einsum(
        "scgl,slr->rscg", alm, legendre, preferred_element_type=jnp.float32
    )
    both = lax.all_gather(own, "half", axis=3, tiled=True)
    mixed = jnp.einsum("fg,rscg->rscf", field_mix, both, precision=highest).astype(jnp.bfloat16)
    by_cycle = lax.all_to_all(mixed, "dev", split_axis=0, concat_axis=1, tiled=True)
    cycle_count, order_count, _, field_count = by_cycle.shape
    weights = jnp.where(order_ids == 0, 1.0, 2.0).astype(jnp.float32) / math.sqrt(2.0 * order_count)
    per_cycle = NPHI // TILE
    pieces = jnp.arange(per_cycle, dtype=jnp.int32)
    inner = jnp.arange(TILE, dtype=jnp.int32)
    outer_angle = (order_ids[:, None] * (2 * TILE * pieces[None, :]) % (2 * NPHI)).astype(
        jnp.float32
    ) * (math.pi / NPHI)
    inner_angle = (order_ids[:, None] * (2 * inner[None, :] + 1) % (2 * NPHI)).astype(
        jnp.float32
    ) * (math.pi / NPHI)
    real = by_cycle[:, :, 0].astype(jnp.float32) * weights[None, :, None]
    imag = by_cycle[:, :, 1].astype(jnp.float32) * weights[None, :, None]
    cos_out = jnp.cos(outer_angle).T[None, :, None, :]
    sin_out = jnp.sin(outer_angle).T[None, :, None, :]
    real = real.transpose(0, 2, 1)[:, None]
    imag = imag.transpose(0, 2, 1)[:, None]
    turned = jnp.concatenate(
        [real * cos_out - imag * sin_out, -(real * sin_out + imag * cos_out)], axis=-1
    )
    basis = jnp.concatenate([jnp.cos(inner_angle), jnp.sin(inner_angle)], axis=0)
    map_tiles = jnp.einsum("rafm,mb->rafb", turned, basis, precision=highest).astype(jnp.bfloat16)
    map_tiles = map_tiles.reshape(cycle_count * per_cycle, field_count, TILE)
    tile_count = map_tiles.shape[0]
    slot_capacity = fetch_list.shape[2]
    owner_row = lax.dynamic_index_in_dim(fetch_list, position, 0, keepdims=False)
    outgoing = map_tiles[jnp.maximum(owner_row, 0)]
    fetched = lax.all_to_all(outgoing, "dev", split_axis=0, concat_axis=0, tiled=True)
    slot_total = device_count * slot_capacity
    flat_fetched = fetched.reshape(slot_total, field_count, TILE)
    per_slot = scan_part(
        flat_fetched, scan_tiles, block_tile, block_pix, noise_kernel, scan_weight
    )
    per_slot = per_slot.reshape(device_count, slot_capacity, field_count, TILE)
    returned = lax.all_to_all(per_slot, "dev", split_axis=0, concat_axis=0, tiled=True)
    owner_select = (
        jnp.arange(tile_count, dtype=jnp.int32)[:, None] == owner_row.reshape(-1)[None, :]
    ).astype(jnp.float32)
    own_tiles = jnp.dot(
        owner_select, returned.reshape(slot_total, field_count * TILE), precision=highest
    )
    binned = own_tiles.reshape(cycle_count, NPHI // TILE, field_count, TILE).transpose(0, 2, 1, 3)
    return binned.reshape(cycle_count, field_count, NPHI)


def solution(mesh):
    return jax.shard_map(
        local,
        mesh=mesh,
        in_specs=(
            P("half", None),
            P("dev", None, "half", None),
            P("dev", None, None),
            P(),
            P(),
            P("dev", None),
            P("dev", None),
            P("dev", None),
            P("dev", None),
            P("dev"),
        ),
        out_specs=P("dev", "half", None),
        check_vma=False,
    )
```

time: 159 us -> 69.9 us (0.44)
  local copies, waits for them, and re-layouts: 67.3 us -> 5.33 us
  Pallas kernels: 0 us -> 20.8 us
  other arithmetic: 18.9 us -> 1.36 us
  matrix products: 20.3 us -> 3.9 us
  between operations: 13.7 us -> 0.19 us
  blocking collectives: 0 us -> 12.6 us
  waiting for transfers between devices: 20.5 us -> 13.4 us
  starting transfers between devices: 17.2 us -> 11.8 us
    unnamed x30 -> x18, local copies, waits for them, and re-layouts: 29.8 us -> 3.34 us
    pallas_call x0 -> x1, Pallas kernels: none -> 20.8 us  [scan_part(): pl.pallas_call(scan_kernel, out_shape=jax.ShapeDtypeStruct(tiles.shape, j...]
    reshape x3 -> x0, local copies, waits for them, and re-layouts: 20.2 us -> none  [the longest x2 20.2 us: toeplitz_rows(): repeated[:, :block_len * (2 * block_len - 1)]]
    dot_general x16 -> x3, matrix products: 20 us -> 3.54 us  [the longest x1 2.36 us: local(): jnp.einsum('scgl,slr->rscg', alm, legendre, preferred_element_type=jnp.fl...]
    all_to_all x0 -> x1, blocking collectives: none -> 10.5 us  [local(): lax.all_to_all(outgoing, 'dev', split_axis=0, concat_axis=0, tiled=True)]
    another operation x8 -> x0, other arithmetic: 10.2 us -> none
    slice x3 -> x0, local copies, waits for them, and re-layouts: 6.55 us -> none  [the longest x2 6.47 us: toeplitz_rows(): repeated[:, :block_len * (2 * block_len - 1)]]
    all_gather x1 -> x0, waiting for transfers between devices: 6.09 us -> none  [local(): both_halves = lax.all_gather(alm, 'half', axis=2, tiled=True)]
  transfers between devices with their start and end apart: 4 -> 2, of which waited for: 3 -> 2; matrix products, arithmetic and copies ran while one was open for 38% -> 2% of each run, Pallas kernels for 0% -> 0%
where the time goes in v1:
time: 69.9 us; the launch traced here: 69.4 us
  Pallas kernels  20.8 us (30%)
  waiting for transfers between devices  13.4 us (19%)
  blocking collectives  12.6 us (18%)
  starting transfers between devices  11.8 us (17%)
  local copies, waits for them, and re-layouts  5.33 us (8%)
  matrix products  3.9 us (6%)
  other arithmetic  1.36 us (2%)
    pallas_call x1, Pallas kernels, scan_part(): pl.pallas_call(scan_kernel, out_shape=jax.ShapeDtypeStruct(tiles.shape, j...  20.8 us
    all_to_all x1, blocking collectives, local(): lax.all_to_all(outgoing, 'dev', split_axis=0, concat_axis=0, tiled=True)  10.5 us
    all_to_all x1, waiting for transfers between devices, local(): lax.all_to_all(per_slot, 'dev', split_axis=0, concat_axis=0, tiled=True)  8.29 us
    all_to_all x1, starting transfers between devices, local(): lax.all_to_all(mixed, 'dev', split_axis=0, concat_axis=1, tiled=True)  8.22 us
    all_to_all x1, waiting for transfers between devices, local(): lax.all_to_all(mixed, 'dev', split_axis=0, concat_axis=1, tiled=True)  5.14 us
    all_to_all x1, starting transfers between devices, local(): lax.all_to_all(per_slot, 'dev', split_axis=0, concat_axis=0, tiled=True)  3.53 us
    unnamed x18, local copies, waits for them, and re-layouts  3.34 us
    dot_general x1, matrix products, local(): jnp.einsum('scgl,slr->rscg', alm, legendre, preferred_element_type=jnp.fl...  2.36 us
  transfers between devices with their start and end apart: 2, of which 2 were waited for; matrix products, arithmetic and copies ran while one was open for 2% of the time, Pallas kernels for 0%

profile of v1, /device:TPU:0, one launch (start us, length us, event | category | flops | bytes accessed | tf_op | source)
XLA Modules:
  0.0 69.4 jit_solution(10730193942913867247)
XLA Ops:
  0.0 0.0 copy-start
  0.0 1.2 %copy-done = bf16[8,2,16,2048]{3,2,1,0:T(8,128)(2,1)S(1)} copy-done((bf16[8,2,16,2048]{3,2,1,0:T(8,128)(2,1)S(1)}, bf16[8,2,16,2048]{3,2,1,0:T(8,128)(2,1)}, u32[]{:S(2)}) %copy-start) | copy-done | bytes 1048600
  1.2 2.4 %convolution_bitcast_fusion.1 = f32[16,8,2,16]{3,0,2,1:T(8,128)S(1)} fusion(bf16[8,2,16,2048]{3,2,1,0:T(8,128)(2,1)S(1)} %copy-done, bf16[8,2048,16]{1,2,0:T(8,128)(2,1)} %param.12), kind=kOutput, calls=%fused_computation.3 | convolution fusion | flops 16777216 | bytes 1589248 | tf_op jit(solution)/shard_map/scgl,slr->rscg/dot_general | solution.py:160
  3.6 0.1 copy.20
  3.7 0.0 copy-start.6
  3.7 2.1 %all_gather.3 = f32[16,8,2,32]{0,1,2,3:T(8,128)S(1)} all-gather(f32[16,8,2,16]{0,1,2,3:T(8,128)S(1)} %copy.20), channel_id=1, replica_groups=mesh['half'=2,'dev'=16] {'half'}, dimensions={3}, use_global_device_ids=true | all-gather | bytes 49152 | tf_op jit(solution)/shard_map/all_gather | solution.py:163
  5.8 0.0 copy-done.6
  5.8 0.6 convolution_convert_fusion.1
  6.4 0.1 copy.22
  6.5 0.7 %reshape.307 = bf16[16,2,128]{2,1,0:T(2,128)(2,1)} reshape(bf16[16,8,2,16]{3,2,1,0:T(2,128)(2,1)S(1)} %copy.22) | data formatting | bytes 16384
  7.2 8.2 %all-to-all-start = ((bf16[16,2,128]{2,1,0:T(2,128)(2,1)}), bf16[16,2,128]{2,1,0:T(2,128)(2,1)S(1)}, u32[]{:S(2)}, u32[]{:S(2)}) async-start(bf16[16,2,128]{2,1,0:T(2,128)(2,1)} %reshape.307), calls=%async_computation | async-start | bytes 16384 | tf_op jit(solution)/shard_map/all_to_all | solution.py:165
  15.4 0.0 copy-start.7
  15.5 0.6 copy-done.7
  16.1 0.1 fusion.22
  16.3 0.3 fusion.14
  16.6 0.7 broadcast_maximum_fusion
  17.3 0.1 copy.26
  17.4 0.1 reshape.295
  17.5 5.1 %all-to-all-done = bf16[16,2,128]{2,1,0:T(2,128)(2,1)S(1)} async-done(((bf16[16,2,128]{2,1,0:T(2,128)(2,1)}), bf16[16,2,128]{2,1,0:T(2,128)(2,1)S(1)}, u32[]{:S(2)}, u32[]{:S(2)}) %all-to-all-start) | async-done | bytes 8224 | tf_op jit(solution)/shard_map/all_to_all | solution.py:165
  22.6 0.1 reshape.308
  22.7 0.1 fusion.12
  22.8 0.1 copy.24
  22.9 0.1 copy.25
  23.0 0.1 multiply_subtract_fusion
  23.0 0.6 convolution_convert_fusion
  23.6 0.0 copy-start.1
  23.6 0.6 gather_fusion
  24.2 0.0 copy-start.2
  24.3 0.0 copy-start.3
  24.3 0.0 copy-start.4
  24.3 10.5 %all_to_all.22 = bf16[16,2,16,128]{3,2,1,0:T(8,128)(2,1)S(1)} all-to-all(bf16[16,2,16,128]{3,2,1,0:T(8,128)(2,1)S(1)} %bitcast.70), channel_id=1, replica_groups=mesh['half'=2,'dev'=16] {'dev'}, dimensions={0} | all-to-all | bytes 262144 | tf_op jit(solution)/shard_map/all_to_all | solution.py:193
  34.8 0.0 copy-start.5
  34.8 0.0 copy-done.1
  34.8 0.0 copy-done.2
  34.8 0.0 copy-done.3
  34.8 0.0 copy-done.4
  34.8 0.6 copy-done.5
  35.5 20.8 %scans.1 = f32[32,16,128]{2,1,0:T(8,128)} custom-call(s32[4,32]{1,0:T(4,128)S(1)} %copy-done.3, s32[4,32]{1,0:T(4,128)S(1)} %copy-done.4, f32[4]{0:T(128)S(1)} %copy-done.5, bf16[32,16,128]{2,1,0:T(8,128)(2,1)S(1)} %bitcast.68, s32[4,16384]{1,0:T(4,128)S(1)} %copy-done.1, f32[4,512]{1,0:T(4,128)S(1)} %copy-done.2), custom_call_target="tpu_custom_call" | custom-call | tf_op jit(solution)/shard_map/scans/pallas_call | solution.py:130
  56.3 3.5 %all-to-all-start.2 = ((f32[16,2,16,128]{3,2,1,0:T(8,128)}), f32[16,2,16,128]{3,2,1,0:T(8,128)S(1)}, u32[]{:S(2)}, u32[]{:S(2)}) async-start(f32[16,2,16,128]{3,2,1,0:T(8,128)} %bitcast.18), calls=%async_computation.2 | async-start | bytes 524288 | tf_op jit(solution)/shard_map/all_to_all | solution.py:200
  59.8 0.1 copy.19
  59.9 0.1 eq.42
  60.0 8.3 %all-to-all-done.2 = f32[16,2,16,128]{3,2,1,0:T(8,128)S(1)} async-done(((f32[16,2,16,128]{3,2,1,0:T(8,128)}), f32[16,2,16,128]{3,2,1,0:T(8,128)S(1)}, u32[]{:S(2)}, u32[]{:S(2)}) %all-to-all-start.2) | async-done | bytes 262176 | tf_op jit(solution)/shard_map/all_to_all | solution.py:200
  68.3 0.4 convolution_bitcast_fusion
  68.7 0.8 %reshape.290 = f32[1,16,4096]{2,1,0:T(8,128)} reshape(f32[1,16,32,128]{3,2,1,0:T(8,128)S(1)} %convolution_bitcast_fusion) | data formatting | bytes 524288 | tf_op jit(solution)/shard_map/reshape | solution.py:208
  (5 shorter events, 0.0 us)
Async XLA Ops:
  0.0 1.2 %copy-start = (bf16[8,2,16,2048]{3,2,1,0:T(8,128)(2,1)S(1)}, bf16[8,2,16,2048]{3,2,1,0:T(8,128)(2,1)}, u32[]{:S(2)}) copy-start(bf16[8,2,16,2048]{3,2,1,0:T(8,128)(2,1)} %param.11) | copy-start | bytes 3145732
  3.7 2.1 %copy-start.6 = (f32[16,32]{1,0:T(8,128)S(1)}, f32[16,32]{1,0:T(8,128)}, u32[]{:S(2)}) copy-start(f32[16,32]{1,0:T(8,128)} %param.10) | copy-start | bytes 6148
  7.2 15.4 %all-to-all-start = ((bf16[16,2,128]{2,1,0:T(2,128)(2,1)}), bf16[16,2,128]{2,1,0:T(2,128)(2,1)S(1)}, u32[]{:S(2)}, u32[]{:S(2)}) async-start(bf16[16,2,128]{2,1,0:T(2,128)(2,1)} %reshape.307), calls=%async_computation | async-start | bytes 16384 | tf_op jit(solution)/shard_map/all_to_all | solution.py:165
  15.4 0.7 copy-start.7
  23.6 11.2 %copy-start.1 = (s32[4,16384]{1,0:T(4,128)S(1)}, s32[4,16384]{1,0:T(4,128)}, u32[]{:S(2)}) copy-start(s32[4,16384]{1,0:T(4,128)} %pix.1) | copy-start | bytes 786436
  24.2 10.6 %copy-start.2 = (f32[4,512]{1,0:T(4,128)S(1)}, f32[4,512]{1,0:T(4,128)}, u32[]{:S(2)}) copy-start(f32[4,512]{1,0:T(4,128)} %noise.1) | copy-start | bytes 24580
  24.3 10.6 %copy-start.3 = (s32[4,32]{1,0:T(4,128)S(1)}, s32[4,32]{1,0:T(4,128)}, u32[]{:S(2)}) copy-start(s32[4,32]{1,0:T(4,128)} %scan_tiles.1) | copy-start | bytes 1540
  24.3 10.5 %copy-start.4 = (s32[4,32]{1,0:T(4,128)S(1)}, s32[4,32]{1,0:T(4,128)}, u32[]{:S(2)}) copy-start(s32[4,32]{1,0:T(4,128)} %block_tile.1) | copy-start | bytes 1540
  34.8 0.7 copy-start.5
  56.3 12.0 %all-to-all-start.2 = ((f32[16,2,16,128]{3,2,1,0:T(8,128)}), f32[16,2,16,128]{3,2,1,0:T(8,128)S(1)}, u32[]{:S(2)}, u32[]{:S(2)}) async-start(f32[16,2,16,128]{3,2,1,0:T(8,128)} %bitcast.18), calls=%async_computation.2 | async-start | bytes 524288 | tf_op jit(solution)/shard_map/all_to_all | solution.py:200

commit v2 on v1

--- a/solution.py
+++ b/solution.py
@@ -16,7 +16,7 @@
 
 
 def scan_kernel(
-    scan_tiles, block_tile, scan_weight, tiles, pix, noise, out, table, padded
+    scan_tiles, block_tile, scan_weight, tiles, pix, noise, out, table, padded, sums
 ):
     scan_count, block_total = block_tile.shape
     length = pix.shape[1]
@@ -32,7 +32,7 @@
         chunk_blocks //= 2
     chunk_rows = chunk_blocks * per_block * fields
 
-    out[...] = jnp.zeros(out.shape, out.dtype)
+    sums[...] = jnp.zeros(sums.shape, sums.dtype)
     padded[pl.ds(0, halo * fields), :] = jnp.zeros((halo * fields, COLS), padded.dtype)
     padded[pl.ds(halo * fields + rows, halo * fields), :] = jnp.zeros(
         (halo * fields, COLS), padded.dtype
@@ -114,13 +114,14 @@
                     row, hot, (((1,), (1,)), ((), ())), preferred_element_type=jnp.float32
                 )
                 slot = scan_tiles[n, block_tile[n, b]]
-                out[slot] += part
+                sums[slot] += part
             return carry
 
         lax.fori_loop(0, block_total // chunk_blocks, chunk, 0)
 
     for n in range(scan_count):
         one_scan(n)
+    out[...] = sums[...].astype(out.dtype)
 
 
 def scan_part(tiles, scan_tiles, block_tile, block_pix, noise_kernel, scan_weight):
@@ -129,16 +130,299 @@
     length = block_pix.shape[1]
     return pl.pallas_call(
         scan_kernel,
-        out_shape=jax.ShapeDtypeStruct(tiles.shape, jnp.float32),
+        out_shape=jax.ShapeDtypeStruct(tiles.shape, jnp.bfloat16),
         in_specs=[pl.BlockSpec(memory_space=SMEM)] * 3 + [pl.BlockSpec(memory_space=VMEM)] * 3,
         out_specs=pl.BlockSpec(memory_space=VMEM),
         scratch_shapes=[
             VMEM((scan_count, 2 * lags + COLS, COLS), jnp.bfloat16),
             VMEM(((length + 2 * lags) // COLS * fields, COLS), jnp.bfloat16),
+            VMEM(tiles.shape, jnp.float32),
         ],
         compiler_params=pltpu.CompilerParams(vmem_limit_bytes=40 * 2**20),
         name="scans",
     )(scan_tiles, block_tile, scan_weight, tiles, block_pix, noise_kernel)
+
+
+MESH = pl.DeviceIdType.MESH
+HIGHEST = lax.Precision.HIGHEST
+SIDES = (((1,), (1,)), ((), ()))
+
+
+def cos_sin(steps):
+    quarter = NPHI // 2
+    turn = (steps + quarter // 2) // quarter
+    x = (steps - turn * quarter).astype(jnp.float32) * (math.pi / NPHI)
+    y = x * x
+    sin = x * (1 + y * (-1 / 6 + y * (1 / 120 + y * (-1 / 5040 + y / 362880))))
+    cos = 1 + y * (-1 / 2 + y * (1 / 24 + y * (-1 / 720 + y * (1 / 40320 - y / 3628800))))
+    odd = turn % 2 == 1
+    cos_sign = jnp.where((turn == 1) | (turn == 2), -1.0, 1.0)
+    sin_sign = jnp.where((turn == 2) | (turn == 3), -1.0, 1.0)
+    return jnp.where(odd, sin, cos) * cos_sign, jnp.where(odd, cos, sin) * sin_sign
+
+
+def meet(count, peer):
+    barrier = pltpu.get_barrier_semaphore()
+
+    def greet(i, carry):
+        pl.semaphore_signal(barrier, inc=1, device_id=peer(i), device_id_type=MESH)
+        return carry
+
+    lax.fori_loop(1, count, greet, 0)
+    return lambda: pl.semaphore_wait(barrier, count - 1)
+
+
+def map_kernel(
+    owner, orders, mix, alm, legendre, out, coeff_out, coeff_in, tiles, tiles_out, tiles_in,
+    sent, got, tile_sent, tile_got,
+):
+    half, dev = lax.axis_index("half"), lax.axis_index("dev")
+    halves, devs = lax.axis_size("half"), lax.axis_size("dev")
+    everyone = halves * devs
+    mine = half * devs + dev
+    fields = mix.shape[0]
+    caps = owner.shape[0]
+    cycles = coeff_out.shape[0]
+    groups = coeff_out.shape[1]
+    slots = alm.shape[0] // (2 * fields)
+
+    def any_peer(i):
+        other = lax.rem(mine + i, everyone)
+        return {"half": other // devs, "dev": lax.rem(other, devs)}
+
+    ready = meet(everyone, any_peer)
+    full = lax.dot_general(legendre[...], alm[...], SIDES, preferred_element_type=jnp.float32)
+    lane = lax.broadcasted_iota(jnp.int32, (cycles, full.shape[1]), 1) // (2 * fields)
+    own = jnp.zeros((cycles, full.shape[1]), jnp.float32)
+    for s in range(slots):
+        own = jnp.where(lane == s, full[s * cycles : (s + 1) * cycles], own)
+    for q in range(groups):
+        coeff_out[:, q, :] = own[:, q * TILE : (q + 1) * TILE]
+    ready()
+
+    def coeff_copy(target_half, target_dev, from_half, from_dev, n_out, n_in):
+        return pltpu.make_async_remote_copy(
+            src_ref=coeff_out.at[target_dev],
+            dst_ref=coeff_in.at[from_half, from_dev],
+            send_sem=sent.at[n_out],
+            recv_sem=got.at[n_in],
+            device_id={"half": target_half, "dev": target_dev},
+            device_id_type=MESH,
+        )
+
+    def send_coeff(i, carry):
+        other = lax.rem(mine + i, everyone)
+        coeff_copy(other // devs, lax.rem(other, devs), half, dev, other, mine).start()
+        return carry
+
+    lax.fori_loop(1, everyone, send_coeff, 0)
+    coeff_in[half, dev] = coeff_out[dev]
+
+    ids = orders[...]
+    total = ids.shape[1]
+    per_cycle = NPHI // TILE
+    weight = jnp.where(ids == 0, 1.0, 2.0) / math.sqrt(2.0 * total)
+    outer = lax.broadcasted_iota(jnp.int32, (per_cycle, total), 0) * (2 * TILE)
+    inner = lax.broadcasted_iota(jnp.int32, (TILE, total), 0) * 2 + 1
+    cos_out, sin_out = cos_sin(outer * ids % (2 * NPHI))
+    basis = jnp.concatenate(cos_sin(inner * ids % (2 * NPHI)), axis=1)
+    spread = []
+    row_field = lax.broadcasted_iota(jnp.int32, (2 * fields, fields), 0) % fields
+    pick_row = row_field == lax.broadcasted_iota(jnp.int32, (2 * fields, fields), 1)
+    wide = (2 * fields, TILE)
+    same = lax.broadcasted_iota(jnp.int32, wide, 0) // fields == (
+        lax.broadcasted_iota(jnp.int32, wide, 1) // fields
+    ) % 2
+    for h in range(halves):
+        lanes = (mix.shape[1], TILE)
+        pick_lane = lax.broadcasted_iota(jnp.int32, lanes, 0) == (
+            lax.broadcasted_iota(jnp.int32, lanes, 1) % fields + h * fields
+        )
+        rows = jnp.dot(
+            pick_row.astype(jnp.float32), mix[...], precision=HIGHEST,
+            preferred_element_type=jnp.float32,
+        )
+        rows = jnp.dot(
+            rows, pick_lane.astype(jnp.float32), precision=HIGHEST,
+            preferred_element_type=jnp.float32,
+        )
+        spread.append(jnp.where(same, rows, 0.0))
+
+    def wait_coeff(i, carry):
+        other = lax.rem(mine + i, everyone)
+        copy = coeff_copy(
+            other // devs, lax.rem(other, devs), other // devs, lax.rem(other, devs), other, other
+        )
+        copy.wait_recv()
+        copy.wait_send()
+        return carry
+
+    lax.fori_loop(1, everyone, wait_coeff, 0)
+    coeff = jnp.zeros((2 * fields, total), jnp.float32)
+    per_group = slots // groups
+    for h in range(halves):
+        block = jnp.concatenate([coeff_in[h, :, q, :] for q in range(groups)], axis=0)
+        group = lax.broadcasted_iota(jnp.int32, block.shape, 1) // (2 * fields)
+        block = jnp.concatenate(
+            [jnp.where(group == s, block, 0.0) for s in range(per_group)], axis=0
+        )
+        coeff = coeff + lax.dot_general(
+            spread[h], block, SIDES, precision=HIGHEST, preferred_element_type=jnp.float32
+        )
+    coeff = coeff * weight
+    real, imag = coeff[:fields], coeff[fields:]
+    turned = []
+    for a in range(per_cycle):
+        c, s = cos_out[a : a + 1], sin_out[a : a + 1]
+        turned.append(jnp.concatenate([real * c - imag * s, -(real * s + imag * c)], axis=1))
+    pixels = lax.dot_general(
+        jnp.concatenate(turned, axis=0), basis, SIDES, precision=HIGHEST,
+        preferred_element_type=jnp.float32,
+    ).astype(jnp.bfloat16)
+    for a in range(per_cycle):
+        tiles[a] = pixels[a * fields : (a + 1) * fields]
+
+    def tile_copy(target, source):
+        return pltpu.make_async_remote_copy(
+            src_ref=tiles_out.at[target],
+            dst_ref=tiles_in.at[source],
+            send_sem=tile_sent.at[target],
+            recv_sem=tile_got.at[source],
+            device_id={"half": half, "dev": target},
+            device_id_type=MESH,
+        )
+
+    def send_tiles(i, carry):
+        other = lax.rem(dev + i, devs)
+        for k in range(caps):
+            tiles_out[other, k] = tiles[jnp.maximum(owner[k, other], 0)]
+        tile_copy(other, dev).start()
+        return carry
+
+    lax.fori_loop(1, devs, send_tiles, 0)
+    for k in range(caps):
+        tiles_in[dev, k] = tiles[jnp.maximum(owner[k, dev], 0)]
+
+    def wait_tiles(i, carry):
+        other = lax.rem(dev + i, devs)
+        pltpu.make_async_remote_copy(
+            src_ref=tiles_out.at[other],
+            dst_ref=tiles_in.at[other],
+            send_sem=tile_sent.at[other],
+            recv_sem=tile_got.at[other],
+            device_id={"half": half, "dev": other},
+            device_id_type=MESH,
+        ).wait()
+        return carry
+
+    lax.fori_loop(1, devs, wait_tiles, 0)
+    out[...] = tiles_in[...]
+
+
+def map_part(owner, orders, field_mix, alm, legendre, devs, halves):
+    caps = owner.shape[0]
+    fields = field_mix.shape[0]
+    groups = alm.shape[0] // TILE
+    cycles = legendre.shape[0] * 2 * fields // alm.shape[0]
+    return pl.pallas_call(
+        map_kernel,
+        out_shape=jax.ShapeDtypeStruct((devs, caps, fields, TILE), jnp.bfloat16),
+        in_specs=[pl.BlockSpec(memory_space=SMEM)] + [pl.BlockSpec(memory_space=VMEM)] * 4,
+        out_specs=pl.BlockSpec(memory_space=VMEM),
+        scratch_shapes=[
+            VMEM((cycles, groups, TILE), jnp.float32),
+            VMEM((halves, devs, groups, TILE), jnp.float32),
+            VMEM((NPHI // TILE, fields, TILE), jnp.bfloat16),
+            VMEM((devs, caps, fields, TILE), jnp.bfloat16),
+            VMEM((devs, caps, fields, TILE), jnp.bfloat16),
+            pltpu.SemaphoreType.DMA((halves * devs,)),
+            pltpu.SemaphoreType.DMA((halves * devs,)),
+            pltpu.SemaphoreType.DMA((devs,)),
+            pltpu.SemaphoreType.DMA((devs,)),
+        ],
+        compiler_params=pltpu.CompilerParams(
+            collective_id=0, has_side_effects=True, vmem_limit_bytes=48 * 2**20
+        ),
+        name="maps",
+    )(owner, orders, field_mix, alm, legendre)
+
+
+def return_kernel(parts, out, held, sent, got):
+    half, dev = lax.axis_index("half"), lax.axis_index("dev")
+    devs = lax.axis_size("dev")
+
+    def peer(i):
+        return {"half": half, "dev": lax.rem(dev + i, devs)}
+
+    meet(devs, peer)()
+
+    def copy(target, source):
+        return pltpu.make_async_remote_copy(
+            src_ref=parts.at[target],
+            dst_ref=held.at[source],
+            send_sem=sent.at[target],
+            recv_sem=got.at[source],
+            device_id={"half": half, "dev": target},
+            device_id_type=MESH,
+        )
+
+    def send(i, carry):
+        copy(lax.rem(dev + i, devs), dev).start()
+        return carry
+
+    lax.fori_loop(1, devs, send, 0)
+    held[dev] = parts[dev]
+
+    def wait(i, carry):
+        other = lax.rem(dev + i, devs)
+        copy(other, other).wait()
+        return carry
+
+    lax.fori_loop(1, devs, wait, 0)
+    out[...] = held[...]
+
+
+def return_part(parts, devs):
+    return pl.pallas_call(
+        return_kernel,
+        out_shape=jax.ShapeDtypeStruct(parts.shape, parts.dtype),
+        in_specs=[pl.BlockSpec(memory_space=VMEM)],
+        out_specs=pl.BlockSpec(memory_space=VMEM),
+        scratch_shapes=[
+            VMEM(parts.shape, parts.dtype),
+            pltpu.SemaphoreType.DMA((devs,)),
+            pltpu.SemaphoreType.DMA((devs,)),
+        ],
+        compiler_params=pltpu.CompilerParams(
+            collective_id=1, has_side_effects=True, vmem_limit_bytes=32 * 2**20
+        ),
+        name="returns",
+    )(parts)
+
+
+def place_kernel(owner, parts, out):
+    caps = owner.shape[0]
+    out[...] = jnp.zeros(out.shape, out.dtype)
+
+    def one(e, carry):
+        for k in range(caps):
+            tile = owner[k, e]
+            at = pl.ds(pl.multiple_of(jnp.maximum(tile, 0) * TILE, TILE), TILE)
+            out[0, :, at] += jnp.where(tile >= 0, parts[e, k].astype(out.dtype), 0.0)
+        return carry
+
+    lax.fori_loop(0, owner.shape[1], one, 0)
+
+
+def place_part(owner, parts):
+    return pl.pallas_call(
+        place_kernel,
+        out_shape=jax.ShapeDtypeStruct((1, parts.shape[2], NPHI), jnp.float32),
+        in_specs=[pl.BlockSpec(memory_space=SMEM), pl.BlockSpec(memory_space=VMEM)],
+        out_specs=pl.BlockSpec(memory_space=VMEM),
+        compiler_params=pltpu.CompilerParams(vmem_limit_bytes=32 * 2**20),
+        name="placing",
+    )(owner, parts)
 
 
 def local(
@@ -153,59 +437,34 @@
     noise_kernel,
     scan_weight,
 ):
-    highest = lax.Precision.HIGHEST
-    device_count = lax.axis_size("dev")
-    position = lax.axis_index("dev")
+    devs = lax.axis_size("dev")
     halves = lax.axis_size("half")
-    own = jnp.einsum(
-        "scgl,slr->rscg", alm, legendre, preferred_element_type=jnp.float32
+    order_slots, parts, fields, ells = alm.shape
+    cycles = legendre.shape[2]
+    owner = lax.dynamic_index_in_dim(
+        fetch_list.transpose(0, 2, 1), lax.axis_index("dev"), 0, keepdims=False
     )
-    both = lax.all_gather(own, "half", axis=3, tiled=True)
-    mixed = jnp.einsum("fg,rscg->rscf", field_mix, both, precision=highest).astype(jnp.bfloat16)
-    by_cycle = lax.all_to_all(mixed, "dev", split_axis=0, concat_axis=1, tiled=True)
-    cycle_count, order_count, _, field_count = by_cycle.shape
-    weights = jnp.where(order_ids == 0, 1.0, 2.0).astype(jnp.float32) / math.sqrt(2.0 * order_count)
-    per_cycle = NPHI // TILE
-    pieces = jnp.arange(per_cycle, dtype=jnp.int32)
-    inner = jnp.arange(TILE, dtype=jnp.int32)
-    outer_angle = (order_ids[:, None] * (2 * TILE * pieces[None, :]) % (2 * NPHI)).astype(
-        jnp.float32
-    ) * (math.pi / NPHI)
-    inner_angle = (order_ids[:, None] * (2 * inner[None, :] + 1) % (2 * NPHI)).astype(
-        jnp.float32
-    ) * (math.pi / NPHI)
-    real = by_cycle[:, :, 0].astype(jnp.float32) * weights[None, :, None]
-    imag = by_cycle[:, :, 1].astype(jnp.float32) * weights[None, :, None]
-    cos_out = jnp.cos(outer_angle).T[None, :, None, :]
-    sin_out = jnp.sin(outer_angle).T[None, :, None, :]
-    real = real.transpose(0, 2, 1)[:, None]
-    imag = imag.transpose(0, 2, 1)[:, None]
-    turned = jnp.concatenate(
-        [real * cos_out - imag * sin_out, -(real * sin_out + imag * cos_out)], axis=-1
+    per_row = TILE // (parts * fields)
+    orders = order_ids.reshape(devs, order_slots // per_row, per_row).transpose(2, 1, 0)
+    tiles = map_part(
+        owner,
+        orders.reshape(1, -1),
+        field_mix,
+        alm.reshape(order_slots * parts * fields, ells),
+        legendre.transpose(0, 2, 1).reshape(order_slots * cycles, ells),
+        devs,
+        halves,
     )
-    basis = jnp.concatenate([jnp.cos(inner_angle), jnp.sin(inner_angle)], axis=0)
-    map_tiles = jnp.einsum("rafm,mb->rafb", turned, basis, precision=highest).astype(jnp.bfloat16)
-    map_tiles = map_tiles.reshape(cycle_count * per_cycle, field_count, TILE)
-    tile_count = map_tiles.shape[0]
-    slot_capacity = fetch_list.shape[2]
-    owner_row = lax.dynamic_index_in_dim(fetch_list, position, 0, keepdims=False)
-    outgoing = map_tiles[jnp.maximum(owner_row, 0)]
-    fetched = lax.all_to_all(outgoing, "dev", split_axis=0, concat_axis=0, tiled=True)
-    slot_total = device_count * slot_capacity
-    flat_fetched = fetched.reshape(slot_total, field_count, TILE)
     per_slot = scan_part(
-        flat_fetched, scan_tiles, block_tile, block_pix, noise_kernel, scan_weight
+        tiles.reshape((-1,) + tiles.shape[2:]),
+        scan_tiles,
+        block_tile,
+        block_pix,
+        noise_kernel,
+        scan_weight,
     )
-    per_slot = per_slot.reshape(device_count, slot_capacity, field_count, TILE)
-    returned = lax.all_to_all(per_slot, "dev", split_axis=0, concat_axis=0, tiled=True)
-    owner_select = (
-        jnp.arange(tile_count, dtype=jnp.int32)[:, None] == owner_row.reshape(-1)[None, :]
-    ).astype(jnp.float32)
-    own_tiles = jnp.dot(
-        owner_select, returned.reshape(slot_total, field_count * TILE), precision=highest
-    )
-    binned = own_tiles.reshape(cycle_count, NPHI // TILE, field_count, TILE).transpose(0, 2, 1, 3)
-    return binned.reshape(cycle_count, field_count, NPHI)
+    returned = return_part(per_slot.reshape(tiles.shape), devs)
+    return place_part(owner, returned)
 
 
 def solution(mesh):

time: 69.9 us -> 53.9 us (0.77)
  Pallas kernels: 20.8 us -> 48.4 us
  waiting for transfers between devices: 13.4 us -> 0 us
  blocking collectives: 12.6 us -> 0 us
  starting transfers between devices: 11.8 us -> 0 us
  matrix products: 3.9 us -> 0 us
  other arithmetic: 1.36 us -> 0 us
    pallas_call x0 -> x3, Pallas kernels: none -> 28.3 us  [the longest x1 19 us: map_part(): pl.pallas_call(map_kernel, out_shape=jax.ShapeDtypeStruct((devs, caps, fi...]
    all_to_all x2 -> x0, waiting for transfers between devices: 13.4 us -> none  [the longest x1 8.29 us: local(): lax.all_to_all(per_slot, 'dev', split_axis=0, concat_axis=0, tiled=True)]
    all_to_all x2 -> x0, starting transfers between devices: 11.8 us -> none  [the longest x1 8.22 us: local(): lax.all_to_all(mixed, 'dev', split_axis=0, concat_axis=1, tiled=True)]
    all_to_all x1 -> x0, blocking collectives: 10.5 us -> none  [local(): lax.all_to_all(outgoing, 'dev', split_axis=0, concat_axis=0, tiled=True)]
    dot_general x4 -> x0, matrix products: 3.9 us -> none  [the longest x1 2.36 us: local(): jnp.einsum('scgl,slr->rscg', alm, legendre, preferred_element_type=jnp.fl...]
    all_gather x1 -> x0, blocking collectives: 2.09 us -> none  [local(): both = lax.all_gather(own, 'half', axis=3, tiled=True)]
    unnamed x18 -> x20, local copies, waits for them, and re-layouts: 3.34 us -> 4.78 us
  transfers between devices with their start and end apart: 2 -> 0, of which waited for: 2 -> 0; matrix products, arithmetic and copies ran while one was open for 2% -> 0% of each run, Pallas kernels for 0% -> 0%
where the time goes in v2:
time: 53.9 us; the launch traced here: 53.6 us
  Pallas kernels  48.4 us (90%)
  local copies, waits for them, and re-layouts  5.07 us (9%)
    pallas_call x1, Pallas kernels, scan_part(): pl.pallas_call(scan_kernel, out_shape=jax.ShapeDtypeStruct(tiles.shape, j...  20.1 us
    pallas_call x1, Pallas kernels, map_part(): pl.pallas_call(map_kernel, out_shape=jax.ShapeDtypeStruct((devs, caps, fi...  19 us
    pallas_call x1, Pallas kernels, return_part(): pl.pallas_call(return_kernel, out_shape=jax.ShapeDtypeStruct(parts.shape,...  7.79 us
    unnamed x20, local copies, waits for them, and re-layouts  4.78 us
    pallas_call x1, Pallas kernels, place_part(): pl.pallas_call(place_kernel, out_shape=jax.ShapeDtypeStruct((1, parts.sha...  1.5 us

profile of v2, /device:TPU:0, one launch (start us, length us, event | category | flops | bytes accessed | tf_op | source)
XLA Modules:
  0.0 53.6 jit_solution(1010493689691553333)
XLA Ops:
  0.0 0.0 copy-start
  0.0 0.7 %copy-done = s32[16,16,2]{1,2,0:T(2,128)S(1)} copy-done((s32[16,16,2]{1,2,0:T(2,128)S(1)}, s32[16,16,2]{1,2,0:T(2,128)}, u32[]{:S(2)}) %copy-start) | copy-done | bytes 2072
  0.7 0.0 copy-start.9
  0.7 0.7 %copy-done.9 = s32[128]{0:T(128)S(1)} copy-done((s32[128]{0:T(128)S(1)}, s32[128]{0:T(128)}, u32[]{:S(2)}) %copy-start.9) | copy-done | bytes 536
  1.4 0.1 reshape.18
  1.5 0.0 copy-start.4
  1.5 0.1 copy.12
  1.6 0.1 reshape.19.orders
  1.7 0.5 copy-done.4
  2.2 0.0 copy-start.1
  2.2 1.2 %copy-done.1 = bf16[8,2,16,2048]{3,2,1,0:T(8,128)(2,1)S(1)} copy-done((bf16[8,2,16,2048]{3,2,1,0:T(8,128)(2,1)S(1)}, bf16[8,2,16,2048]{3,2,1,0:T(8,128)(2,1)}, u32[]{:S(2)}) %copy-start.1) | copy-done | bytes 1048600
  3.4 0.0 copy-start.2
  3.4 1.0 %copy-done.2 = bf16[8,2048,16]{1,2,0:T(8,128)(2,1)S(1)} copy-done((bf16[8,2048,16]{1,2,0:T(8,128)(2,1)S(1)}, bf16[8,2048,16]{1,2,0:T(8,128)(2,1)}, u32[]{:S(2)}) %copy-start.2) | copy-done | bytes 524312
  4.5 0.0 copy-start.3
  4.5 0.0 copy-start.5
  4.5 0.0 copy-start.6
  4.5 0.0 copy-start.7
  4.5 19.0 %maps.1 = bf16[16,2,16,128]{3,2,1,0:T(8,128)(2,1)S(1)} custom-call(s32[2,16]{1,0:T(2,128)S(1)} %dynamic-slice_bitcast_fusion.owner, s32[1,128]{1,0:T(1,128)S(1)} %reshape.19.orders, f32[16,32]{1,0:T(8,128)S(1)} %copy-done.4, bf16[256,2048]{1,0:T(8,128)(2,1)S(1)} %bitcast.11, bf16[128,2048]{1,0:T(8,128)(2,1)S(1)} %bitcast.13), custom_call_target="tpu_custom_call" | custom-call | tf_op jit(solution)/shard_map/maps/pallas_call | solution.py:327
  23.5 0.0 copy-start.8
  23.5 0.0 copy-done.3
  23.5 0.0 copy-done.5
  23.5 0.0 copy-done.6
  23.5 0.0 copy-done.7
  23.5 0.6 %copy-done.8 = f32[4]{0:T(128)S(1)} copy-done((f32[4]{0:T(128)S(1)}, f32[4]{0:T(128)}, u32[]{:S(2)}) %copy-start.8) | copy-done | bytes 40
  24.1 20.1 %scans.1 = bf16[32,16,128]{2,1,0:T(8,128)(2,1)S(1)} custom-call(s32[4,32]{1,0:T(4,128)S(1)} %copy-done.6, s32[4,32]{1,0:T(4,128)S(1)} %copy-done.7, f32[4]{0:T(128)S(1)} %copy-done.8, bf16[32,16,128]{2,1,0:T(8,128)(2,1)S(1)} %bitcast.14, s32[4,16384]{1,0:T(4,128)S(1)} %copy-done.3, f32[4,512]{1,0:T(4,128)S(1)} %copy-done.5), custom_call_target="tpu_custom_call" | custom-call | tf_op jit(solution)/shard_map/scans/pallas_call | solution.py:131
  44.3 7.8 %returns.1.parts = bf16[16,2,16,128]{3,2,1,0:T(8,128)(2,1)S(1)} custom-call(bf16[16,2,16,128]{3,2,1,0:T(8,128)(2,1)S(1)} %bitcast.12), custom_call_target="tpu_custom_call" | custom-call | tf_op jit(solution)/shard_map/returns/pallas_call | solution.py:386
  52.1 1.5 %placing.1 = f32[1,16,4096]{2,1,0:T(8,128)} custom-call(s32[2,16]{1,0:T(2,128)S(1)} %dynamic-slice_bitcast_fusion.owner, bf16[16,2,16,128]{3,2,1,0:T(8,128)(2,1)S(1)} %returns.1.parts), custom_call_target="tpu_custom_call" | custom-call | tf_op jit(solution)/shard_map/placing/pallas_call | solution.py:418
  (1 shorter events, 0.0 us)
Async XLA Ops:
  0.0 0.7 %copy-start = (s32[16,16,2]{1,2,0:T(2,128)S(1)}, s32[16,16,2]{1,2,0:T(2,128)}, u32[]{:S(2)}) copy-start(s32[16,16,2]{1,2,0:T(2,128)} %param.14) | copy-start | bytes 6148
  0.7 0.7 %copy-start.9 = (s32[128]{0:T(128)S(1)}, s32[128]{0:T(128)}, u32[]{:S(2)}) copy-start(s32[128]{0:T(128)} %param.13) | copy-start | bytes 1540
  1.5 0.7 %copy-start.4 = (f32[16,32]{1,0:T(8,128)S(1)}, f32[16,32]{1,0:T(8,128)}, u32[]{:S(2)}) copy-start(f32[16,32]{1,0:T(8,128)} %mix.1) | copy-start | bytes 6148
  2.2 1.2 %copy-start.1 = (bf16[8,2,16,2048]{3,2,1,0:T(8,128)(2,1)S(1)}, bf16[8,2,16,2048]{3,2,1,0:T(8,128)(2,1)}, u32[]{:S(2)}) copy-start(bf16[8,2,16,2048]{3,2,1,0:T(8,128)(2,1)} %param.11) | copy-start | bytes 3145732
  3.4 1.0 %copy-start.2 = (bf16[8,2048,16]{1,2,0:T(8,128)(2,1)S(1)}, bf16[8,2048,16]{1,2,0:T(8,128)(2,1)}, u32[]{:S(2)}) copy-start(bf16[8,2048,16]{1,2,0:T(8,128)(2,1)} %param.12) | copy-start | bytes 1572868
  4.5 19.0 %copy-start.3 = (s32[4,16384]{1,0:T(4,128)S(1)}, s32[4,16384]{1,0:T(4,128)}, u32[]{:S(2)}) copy-start(s32[4,16384]{1,0:T(4,128)} %pix.1) | copy-start | bytes 786436
  4.5 19.0 %copy-start.5 = (f32[4,512]{1,0:T(4,128)S(1)}, f32[4,512]{1,0:T(4,128)}, u32[]{:S(2)}) copy-start(f32[4,512]{1,0:T(4,128)} %noise.1) | copy-start | bytes 24580
  4.5 19.1 %copy-start.6 = (s32[4,32]{1,0:T(4,128)S(1)}, s32[4,32]{1,0:T(4,128)}, u32[]{:S(2)}) copy-start(s32[4,32]{1,0:T(4,128)} %scan_tiles.1) | copy-start | bytes 1540
  4.5 19.1 %copy-start.7 = (s32[4,32]{1,0:T(4,128)S(1)}, s32[4,32]{1,0:T(4,128)}, u32[]{:S(2)}) copy-start(s32[4,32]{1,0:T(4,128)} %block_tile.1) | copy-start | bytes 1540
  23.5 0.7 %copy-start.8 = (f32[4]{0:T(128)S(1)}, f32[4]{0:T(128)}, u32[]{:S(2)}) copy-start(f32[4]{0:T(128)} %scan_weight.1) | copy-start | bytes 52

commit v3 on v2

--- a/solution.py
+++ b/solution.py
@@ -16,7 +16,7 @@
 
 
 def scan_kernel(
-    scan_tiles, block_tile, scan_weight, tiles, pix, noise, out, table, padded, sums
+    scan_tiles, block_tile, scan_weight, tiles, pix, noise, out, table, even, odd, weighted, sums
 ):
     scan_count, block_total = block_tile.shape
     length = pix.shape[1]
@@ -27,16 +27,12 @@
     halo = lags // COLS
     window = 2 * lags + COLS
     rows = (length // COLS) * fields
-    chunk_blocks = 8
-    while block_total % chunk_blocks:
-        chunk_blocks //= 2
-    chunk_rows = chunk_blocks * per_block * fields
-
     sums[...] = jnp.zeros(sums.shape, sums.dtype)
-    padded[pl.ds(0, halo * fields), :] = jnp.zeros((halo * fields, COLS), padded.dtype)
-    padded[pl.ds(halo * fields + rows, halo * fields), :] = jnp.zeros(
-        (halo * fields, COLS), padded.dtype
-    )
+    padded = (even, odd)
+    edge = jnp.zeros((halo * fields, COLS), jnp.bfloat16)
+    for ref in padded:
+        ref[: halo * fields, :] = edge
+        ref[halo * fields + rows :, :] = edge
     taps = noise[...].astype(jnp.bfloat16).astype(jnp.float32)
     lane = lax.broadcasted_iota(jnp.int32, taps.shape, 1)
     moved = jnp.where(lane == lags - 1, 0.0, pltpu.roll(taps, lags - 1, 1))
@@ -66,61 +62,70 @@
             start = top - q * TILE
             table[n, q * TILE : (q + 1) * TILE, :] = strip[:, start : start + COLS]
 
-    def one_scan(n):
-        def sample(b, carry):
-            slot = scan_tiles[n, block_tile[n, b]]
-            tile = tiles[slot].astype(jnp.float32)
-            for c in range(block_len // TILE):
-                at = pl.multiple_of(b * block_len + c * TILE, TILE)
-                index = jnp.broadcast_to(pix[n : n + 1, pl.ds(at, TILE)], tile.shape)
-                value = jnp.take_along_axis(
-                    tile, jnp.maximum(index, 0), axis=1, mode="promise_in_bounds"
-                )
-                value = jnp.where(index >= 0, value, 0.0).astype(padded.dtype)
-                row = pl.multiple_of((b * per_block + (c * TILE) // COLS + halo) * fields, 16)
-                lane_at = (c * TILE) % COLS
-                padded[pl.ds(row, fields), lane_at : lane_at + TILE] = value
+    below = lax.broadcasted_iota(jnp.int32, (TILE, block_len), 0).astype(jnp.float32).astype(
+        jnp.bfloat16
+    )
+
+    def sample(n, b):
+        slot = scan_tiles[n, block_tile[n, b]]
+        tile = tiles[slot].astype(jnp.float32)
+        for c in range(block_len // TILE):
+            at = pl.multiple_of(b * block_len + c * TILE, TILE)
+            index = jnp.broadcast_to(pix[n : n + 1, pl.ds(at, TILE)], tile.shape)
+            value = jnp.take_along_axis(
+                tile, jnp.maximum(index, 0), axis=1, mode="promise_in_bounds"
+            )
+            value = jnp.where(index >= 0, value, 0.0).astype(jnp.bfloat16)
+            row = pl.multiple_of((b * per_block + (c * TILE) // COLS + halo) * fields, 16)
+            lane_at = (c * TILE) % COLS
+            padded[n % 2][pl.ds(row, fields), lane_at : lane_at + TILE] = value
+
+    def collect(n, b):
+        at = pl.multiple_of(b * block_len, TILE)
+        index = pix[n : n + 1, pl.ds(at, block_len)].astype(jnp.float32).astype(jnp.bfloat16)
+        hot = jnp.where(
+            below == index, jnp.ones((), jnp.bfloat16), jnp.zeros((), jnp.bfloat16)
+        )
+        row = jnp.concatenate(
+            [
+                weighted[pl.ds(pl.multiple_of((b * per_block + i) * fields, 16), fields), :]
+                for i in range(per_block)
+            ],
+            axis=1,
+        )
+        part = lax.dot_general(
+            row, hot, (((1,), (1,)), ((), ())), preferred_element_type=jnp.float32
+        )
+        slot = scan_tiles[n, block_tile[n, b]]
+        sums[slot] += part
+
+    def together(step, group):
+        def body(m, carry):
+            for k in range(group):
+                step(m * group + k)
             return carry
 
-        lax.fori_loop(0, block_total, sample, 0, unroll=4)
-        weight = scan_weight[n]
-
-        def chunk(m, carry):
-            base = m * chunk_rows
-            pieces = [
-                padded[pl.ds(pl.multiple_of(base + o * fields, 16), chunk_rows), :]
-                for o in range(2 * halo + 1)
-            ]
-            filtered = jnp.dot(
-                jnp.concatenate(pieces, axis=1), table[n], preferred_element_type=jnp.float32
-            )
-            weighted = (weight * filtered).astype(jnp.bfloat16)
-            for k in range(chunk_blocks):
-                b = m * chunk_blocks + k
-                at = pl.multiple_of(b * block_len, TILE)
-                index = pix[n : n + 1, pl.ds(at, block_len)]
-                hot = (
-                    lax.broadcasted_iota(jnp.int32, (TILE, block_len), 0) == index
-                ).astype(jnp.float32).astype(jnp.bfloat16)
-                first = k * per_block * fields
-                row = jnp.concatenate(
-                    [
-                        weighted[first + i * fields : first + (i + 1) * fields]
-                        for i in range(per_block)
-                    ],
-                    axis=1,
-                )
-                part = lax.dot_general(
-                    row, hot, (((1,), (1,)), ((), ())), preferred_element_type=jnp.float32
-                )
-                slot = scan_tiles[n, block_tile[n, b]]
-                sums[slot] += part
-            return carry
-
-        lax.fori_loop(0, block_total // chunk_blocks, chunk, 0)
-
+        lax.fori_loop(0, block_total // group, body, 0)
+
+    group = 4
+    while block_total % group:
+        group //= 2
+    together(lambda b: sample(0, b), group)
     for n in range(scan_count):
-        one_scan(n)
+        pieces = [
+            padded[n % 2][o * fields : o * fields + rows, :] for o in range(2 * halo + 1)
+        ]
+        filtered = jnp.dot(
+            jnp.concatenate(pieces, axis=1), table[n], preferred_element_type=jnp.float32
+        )
+        weighted[...] = (scan_weight[n] * filtered).astype(jnp.bfloat16)
+
+        def step(b):
+            collect(n, b)
+            if n + 1 < scan_count:
+                sample(n + 1, b)
+
+        together(step, group)
     out[...] = sums[...].astype(out.dtype)
 
 
@@ -136,6 +141,8 @@
         scratch_shapes=[
             VMEM((scan_count, 2 * lags + COLS, COLS), jnp.bfloat16),
             VMEM(((length + 2 * lags) // COLS * fields, COLS), jnp.bfloat16),
+            VMEM(((length + 2 * lags) // COLS * fields, COLS), jnp.bfloat16),
+            VMEM((length // COLS * fields, COLS), jnp.bfloat16),
             VMEM(tiles.shape, jnp.float32),
         ],
         compiler_params=pltpu.CompilerParams(vmem_limit_bytes=40 * 2**20),
@@ -173,15 +180,21 @@
 
 
 def map_kernel(
-    owner, orders, mix, alm, legendre, out, coeff_out, coeff_in, tiles, tiles_out, tiles_in,
-    sent, got, tile_sent, tile_got,
+    owner, orders, mix, alm_hbm, legendre_hbm, out, alm, legendre, coeff_out, coeff_in, tiles,
+    tiles_out, tiles_in, loaded, sent, got, tile_sent, tile_got,
 ):
     half, dev = lax.axis_index("half"), lax.axis_index("dev")
     halves, devs = lax.axis_size("half"), lax.axis_size("dev")
     everyone = halves * devs
     mine = half * devs + dev
     fields = mix.shape[0]
-    caps = owner.shape[0]
+    caps = owner.shape[1]
+    loads = [
+        pltpu.make_async_copy(alm_hbm, alm, loaded.at[0]),
+        pltpu.make_async_copy(legendre_hbm, legendre, loaded.at[1]),
+    ]
+    for load in loads:
+        load.start()
     cycles = coeff_out.shape[0]
     groups = coeff_out.shape[1]
     slots = alm.shape[0] // (2 * fields)
@@ -191,6 +204,8 @@
         return {"half": other // devs, "dev": lax.rem(other, devs)}
 
     ready = meet(everyone, any_peer)
+    for load in loads:
+        load.wait()
     full = lax.dot_general(legendre[...], alm[...], SIDES, preferred_element_type=jnp.float32)
     lane = lax.broadcasted_iota(jnp.int32, (cycles, full.shape[1]), 1) // (2 * fields)
     own = jnp.zeros((cycles, full.shape[1]), jnp.float32)
@@ -218,8 +233,16 @@
     lax.fori_loop(1, everyone, send_coeff, 0)
     coeff_in[half, dev] = coeff_out[dev]
 
-    ids = orders[...]
-    total = ids.shape[1]
+    total = orders.shape[1]
+    per_group = slots // groups
+    place = lax.broadcasted_iota(jnp.int32, (total, total), 1)
+    place = place % devs * slots + place // devs % groups * per_group + place // (devs * groups)
+    moves = (lax.broadcasted_iota(jnp.int32, (total, total), 0) == place).astype(jnp.float32)
+    ids = jnp.dot(
+        orders[...].astype(jnp.float32), moves, precision=HIGHEST,
+        preferred_element_type=jnp.float32,
+    )
+    ids = jnp.round(ids).astype(jnp.int32)
     per_cycle = NPHI // TILE
     weight = jnp.where(ids == 0, 1.0, 2.0) / math.sqrt(2.0 * total)
     outer = lax.broadcasted_iota(jnp.int32, (per_cycle, total), 0) * (2 * TILE)
@@ -259,7 +282,6 @@
 
     lax.fori_loop(1, everyone, wait_coeff, 0)
     coeff = jnp.zeros((2 * fields, total), jnp.float32)
-    per_group = slots // groups
     for h in range(halves):
         block = jnp.concatenate([coeff_in[h, :, q, :] for q in range(groups)], axis=0)
         group = lax.broadcasted_iota(jnp.int32, block.shape, 1) // (2 * fields)
@@ -295,13 +317,13 @@
     def send_tiles(i, carry):
         other = lax.rem(dev + i, devs)
         for k in range(caps):
-            tiles_out[other, k] = tiles[jnp.maximum(owner[k, other], 0)]
+            tiles_out[other, k] = tiles[jnp.maximum(owner[dev, k, other], 0)]
         tile_copy(other, dev).start()
         return carry
 
     lax.fori_loop(1, devs, send_tiles, 0)
     for k in range(caps):
-        tiles_in[dev, k] = tiles[jnp.maximum(owner[k, dev], 0)]
+        tiles_in[dev, k] = tiles[jnp.maximum(owner[dev, k, dev], 0)]
 
     def wait_tiles(i, carry):
         other = lax.rem(dev + i, devs)
@@ -320,21 +342,26 @@
 
 
 def map_part(owner, orders, field_mix, alm, legendre, devs, halves):
-    caps = owner.shape[0]
+    caps = owner.shape[1]
     fields = field_mix.shape[0]
     groups = alm.shape[0] // TILE
     cycles = legendre.shape[0] * 2 * fields // alm.shape[0]
     return pl.pallas_call(
         map_kernel,
         out_shape=jax.ShapeDtypeStruct((devs, caps, fields, TILE), jnp.bfloat16),
-        in_specs=[pl.BlockSpec(memory_space=SMEM)] + [pl.BlockSpec(memory_space=VMEM)] * 4,
+        in_specs=[pl.BlockSpec(memory_space=SMEM)]
+        + [pl.BlockSpec(memory_space=VMEM)] * 2
+        + [pl.BlockSpec(memory_space=pltpu.HBM)] * 2,
         out_specs=pl.BlockSpec(memory_space=VMEM),
         scratch_shapes=[
+            VMEM(alm.shape, alm.dtype),
+            VMEM(legendre.shape, legendre.dtype),
             VMEM((cycles, groups, TILE), jnp.float32),
             VMEM((halves, devs, groups, TILE), jnp.float32),
             VMEM((NPHI // TILE, fields, TILE), jnp.bfloat16),
             VMEM((devs, caps, fields, TILE), jnp.bfloat16),
             VMEM((devs, caps, fields, TILE), jnp.bfloat16),
+            pltpu.SemaphoreType.DMA((2,)),
             pltpu.SemaphoreType.DMA((halves * devs,)),
             pltpu.SemaphoreType.DMA((halves * devs,)),
             pltpu.SemaphoreType.DMA((devs,)),
@@ -401,17 +428,18 @@
 
 
 def place_kernel(owner, parts, out):
-    caps = owner.shape[0]
+    caps = owner.shape[1]
+    dev = lax.axis_index("dev")
     out[...] = jnp.zeros(out.shape, out.dtype)
 
     def one(e, carry):
         for k in range(caps):
-            tile = owner[k, e]
+            tile = owner[dev, k, e]
             at = pl.ds(pl.multiple_of(jnp.maximum(tile, 0) * TILE, TILE), TILE)
             out[0, :, at] += jnp.where(tile >= 0, parts[e, k].astype(out.dtype), 0.0)
         return carry
 
-    lax.fori_loop(0, owner.shape[1], one, 0)
+    lax.fori_loop(0, owner.shape[2], one, 0)
 
 
 def place_part(owner, parts):
@@ -441,14 +469,10 @@
     halves = lax.axis_size("half")
     order_slots, parts, fields, ells = alm.shape
     cycles = legendre.shape[2]
-    owner = lax.dynamic_index_in_dim(
-        fetch_list.transpose(0, 2, 1), lax.axis_index("dev"), 0, keepdims=False
-    )
-    per_row = TILE // (parts * fields)
-    orders = order_ids.reshape(devs, order_slots // per_row, per_row).transpose(2, 1, 0)
+    owner = fetch_list.transpose(0, 2, 1)
     tiles = map_part(
         owner,
-        orders.reshape(1, -1),
+        order_ids.reshape(1, -1),
         field_mix,
         alm.reshape(order_slots * parts * fields, ells),
         legendre.transpose(0, 2, 1).reshape(order_slots * cycles, ells),

time: 53.9 us -> 48 us (0.89)
  Pallas kernels: 48.4 us -> 42.6 us
    pallas_call x1, Pallas kernels: 20.1 us -> 13.7 us  [scan_part(): pl.pallas_call(scan_kernel, out_shape=jax.ShapeDtypeStruct(tiles.shape, j...]
where the time goes in v3:
time: 48 us; the launch traced here: 47.6 us
  Pallas kernels  42.6 us (89%)
  local copies, waits for them, and re-layouts  4.96 us (10%)
    pallas_call x1, Pallas kernels, map_part(): pl.pallas_call(map_kernel, out_shape=jax.ShapeDtypeStruct((devs, caps, fi...  19.4 us
    pallas_call x1, Pallas kernels, scan_part(): pl.pallas_call(scan_kernel, out_shape=jax.ShapeDtypeStruct(tiles.shape, j...  13.7 us
    pallas_call x1, Pallas kernels, return_part(): pl.pallas_call(return_kernel, out_shape=jax.ShapeDtypeStruct(parts.shape,...  7.79 us
    unnamed x20, local copies, waits for them, and re-layouts  4.96 us
    pallas_call x1, Pallas kernels, place_part(): pl.pallas_call(place_kernel, out_shape=jax.ShapeDtypeStruct((1, parts.sha...  1.78 us

profile of v3, /device:TPU:0, one launch (start us, length us, event | category | flops | bytes accessed | tf_op | source)
XLA Modules:
  0.0 47.6 jit_solution(660540622159073353)
XLA Ops:
  0.0 0.0 copy-start.8
  0.0 0.7 %copy-done.8 = s32[128]{0:T(128)S(1)} copy-done((s32[128]{0:T(128)S(1)}, s32[128]{0:T(128)}, u32[]{:S(2)}) %copy-start.8) | copy-done | bytes 536
  0.7 0.0 copy-start
  0.7 1.2 %copy-done = bf16[8,2,16,2048]{3,2,1,0:T(8,128)(2,1)S(1)} copy-done((bf16[8,2,16,2048]{3,2,1,0:T(8,128)(2,1)S(1)}, bf16[8,2,16,2048]{3,2,1,0:T(8,128)(2,1)}, u32[]{:S(2)}) %copy-start) | copy-done | bytes 1048600
  1.9 0.0 copy-start.1
  1.9 1.0 %copy-done.1 = bf16[8,2048,16]{1,2,0:T(8,128)(2,1)S(1)} copy-done((bf16[8,2048,16]{1,2,0:T(8,128)(2,1)S(1)}, bf16[8,2048,16]{1,2,0:T(8,128)(2,1)}, u32[]{:S(2)}) %copy-start.1) | copy-done | bytes 524312
  2.9 0.0 copy-start.3
  2.9 0.7 %copy-done.3 = s32[16,16,2]{1,2,0:T(2,128)S(1)} copy-done((s32[16,16,2]{1,2,0:T(2,128)S(1)}, s32[16,16,2]{1,2,0:T(2,128)}, u32[]{:S(2)}) %copy-start.3) | copy-done | bytes 2072
  3.6 0.0 copy-start.4
  3.6 0.7 %copy-done.4 = f32[16,32]{1,0:T(8,128)S(1)} copy-done((f32[16,32]{1,0:T(8,128)S(1)}, f32[16,32]{1,0:T(8,128)}, u32[]{:S(2)}) %copy-start.4) | copy-done | bytes 2072
  4.3 0.0 copy-start.2
  4.3 0.0 copy-start.5
  4.3 0.0 copy-start.6
  4.3 0.0 copy-start.7
  4.3 19.4 %maps.1 = bf16[16,2,16,128]{3,2,1,0:T(8,128)(2,1)S(1)} custom-call(s32[16,2,16]{2,1,0:T(2,128)S(1)} %bitcast.12, s32[1,128]{1,0:T(1,128)S(1)} %bitcast.14, f32[16,32]{1,0:T(8,128)S(1)} %copy-done.4, bf16[256,2048]{1,0:T(8,128)(2,1)S(1)} %bitcast.8, bf16[128,2048]{1,0:T(8,128)(2,1)S(1)} %bitcast.11), custom_call_target="tpu_custom_call" | custom-call | tf_op jit(solution)/shard_map/maps/pallas_call | solution.py:349
  23.7 0.0 copy-start.9
  23.7 0.0 copy-done.2
  23.7 0.0 copy-done.5
  23.8 0.0 copy-done.6
  23.8 0.0 copy-done.7
  23.8 0.6 %copy-done.9 = f32[4]{0:T(128)S(1)} copy-done((f32[4]{0:T(128)S(1)}, f32[4]{0:T(128)}, u32[]{:S(2)}) %copy-start.9) | copy-done | bytes 40
  24.4 13.7 %scans.1 = bf16[32,16,128]{2,1,0:T(8,128)(2,1)S(1)} custom-call(s32[4,32]{1,0:T(4,128)S(1)} %copy-done.6, s32[4,32]{1,0:T(4,128)S(1)} %copy-done.7, f32[4]{0:T(128)S(1)} %copy-done.9, bf16[32,16,128]{2,1,0:T(8,128)(2,1)S(1)} %bitcast.9, s32[4,16384]{1,0:T(4,128)S(1)} %copy-done.2, f32[4,512]{1,0:T(4,128)S(1)} %copy-done.5), custom_call_target="tpu_custom_call" | custom-call | tf_op jit(solution)/shard_map/scans/pallas_call | solution.py:136
  38.1 7.8 %returns.1.parts = bf16[16,2,16,128]{3,2,1,0:T(8,128)(2,1)S(1)} custom-call(bf16[16,2,16,128]{3,2,1,0:T(8,128)(2,1)S(1)} %bitcast.10), custom_call_target="tpu_custom_call" | custom-call | tf_op jit(solution)/shard_map/returns/pallas_call | solution.py:413
  45.9 1.8 %placing.1 = f32[1,16,4096]{2,1,0:T(8,128)} custom-call(s32[16,2,16]{2,1,0:T(2,128)S(1)} %bitcast.13, bf16[16,2,16,128]{3,2,1,0:T(8,128)(2,1)S(1)} %returns.1.parts), custom_call_target="tpu_custom_call" | custom-call | tf_op jit(solution)/shard_map/placing/pallas_call | solution.py:446
Async XLA Ops:
  0.0 0.7 %copy-start.8 = (s32[128]{0:T(128)S(1)}, s32[128]{0:T(128)}, u32[]{:S(2)}) copy-start(s32[128]{0:T(128)} %param.13) | copy-start | bytes 1540
  0.7 1.2 %copy-start = (bf16[8,2,16,2048]{3,2,1,0:T(8,128)(2,1)S(1)}, bf16[8,2,16,2048]{3,2,1,0:T(8,128)(2,1)}, u32[]{:S(2)}) copy-start(bf16[8,2,16,2048]{3,2,1,0:T(8,128)(2,1)} %param.11) | copy-start | bytes 3145732
  1.9 1.0 %copy-start.1 = (bf16[8,2048,16]{1,2,0:T(8,128)(2,1)S(1)}, bf16[8,2048,16]{1,2,0:T(8,128)(2,1)}, u32[]{:S(2)}) copy-start(bf16[8,2048,16]{1,2,0:T(8,128)(2,1)} %param.12) | copy-start | bytes 1572868
  2.9 0.7 %copy-start.3 = (s32[16,16,2]{1,2,0:T(2,128)S(1)}, s32[16,16,2]{1,2,0:T(2,128)}, u32[]{:S(2)}) copy-start(s32[16,16,2]{1,2,0:T(2,128)} %param.14) | copy-start | bytes 6148
  3.6 0.7 %copy-start.4 = (f32[16,32]{1,0:T(8,128)S(1)}, f32[16,32]{1,0:T(8,128)}, u32[]{:S(2)}) copy-start(f32[16,32]{1,0:T(8,128)} %mix.1) | copy-start | bytes 6148
  4.3 19.4 %copy-start.2 = (s32[4,16384]{1,0:T(4,128)S(1)}, s32[4,16384]{1,0:T(4,128)}, u32[]{:S(2)}) copy-start(s32[4,16384]{1,0:T(4,128)} %pix.1) | copy-start | bytes 786436
  4.3 19.4 %copy-start.5 = (f32[4,512]{1,0:T(4,128)S(1)}, f32[4,512]{1,0:T(4,128)}, u32[]{:S(2)}) copy-start(f32[4,512]{1,0:T(4,128)} %noise.1) | copy-start | bytes 24580
  4.3 19.4 %copy-start.6 = (s32[4,32]{1,0:T(4,128)S(1)}, s32[4,32]{1,0:T(4,128)}, u32[]{:S(2)}) copy-start(s32[4,32]{1,0:T(4,128)} %scan_tiles.1) | copy-start | bytes 1540
  4.3 19.4 %copy-start.7 = (s32[4,32]{1,0:T(4,128)S(1)}, s32[4,32]{1,0:T(4,128)}, u32[]{:S(2)}) copy-start(s32[4,32]{1,0:T(4,128)} %block_tile.1) | copy-start | bytes 1540
  23.7 0.7 %copy-start.9 = (f32[4]{0:T(128)S(1)}, f32[4]{0:T(128)}, u32[]{:S(2)}) copy-start(f32[4]{0:T(128)} %scan_weight.1) | copy-start | bytes 52

commit v4 on v3

v4 whole, which is shorter than its diff:
```python
import functools
import math

import jax
import jax.numpy as jnp
from jax import lax
from jax.experimental import pallas as pl
from jax.experimental.pallas import tpu as pltpu
from jax.sharding import PartitionSpec as P

NPHI = 4096
TILE = 128
COLS = 256
VMEM = pltpu.VMEM
SMEM = pltpu.SMEM


MESH = pl.DeviceIdType.MESH
HIGHEST = lax.Precision.HIGHEST
SIDES = (((1,), (1,)), ((), ()))


def cos_sin(steps):
    quarter = NPHI // 2
    turn = (steps + quarter // 2) // quarter
    x = (steps - turn * quarter).astype(jnp.float32) * (math.pi / NPHI)
    y = x * x
    sin = x * (1 + y * (-1 / 6 + y * (1 / 120 + y * (-1 / 5040 + y / 362880))))
    cos = 1 + y * (-1 / 2 + y * (1 / 24 + y * (-1 / 720 + y * (1 / 40320 - y / 3628800))))
    odd = turn % 2 == 1
    cos_sign = jnp.where((turn == 1) | (turn == 2), -1.0, 1.0)
    sin_sign = jnp.where((turn == 2) | (turn == 3), -1.0, 1.0)
    return jnp.where(odd, sin, cos) * cos_sign, jnp.where(odd, cos, sin) * sin_sign


def meet(count, peer):
    barrier = pltpu.get_barrier_semaphore()

    def greet(i, carry):
        pl.semaphore_signal(barrier, inc=1, device_id=peer(i), device_id_type=MESH)
        return carry

    lax.fori_loop(1, count, greet, 0)
    return lambda: pl.semaphore_wait(barrier, count - 1)


def whole_kernel(
    owner, scan_tiles, block_tile, scan_weight, orders_hbm, mix_hbm, alm_hbm, legendre_hbm,
    pix_hbm, noise_hbm, out, orders, mix, alm, legendre, pix, noise, coeff_out, coeff_in, tiles,
    tiles_out, tiles_in, table, even, odd, weighted, parts, sums, back_out, back_in, loaded, sent,
    got, tile_sent, tile_got, back_sent, back_got,
):
    half, dev = lax.axis_index("half"), lax.axis_index("dev")
    halves, devs = lax.axis_size("half"), lax.axis_size("dev")
    everyone = halves * devs
    mine = half * devs + dev
    fields = mix.shape[0]
    caps = owner.shape[1]
    loads = [
        pltpu.make_async_copy(source, target, loaded.at[i])
        for i, (source, target) in enumerate(
            (
                (alm_hbm, alm),
                (legendre_hbm, legendre),
                (orders_hbm, orders),
                (mix_hbm, mix),
                (noise_hbm, noise),
                (pix_hbm, pix),
            )
        )
    ]
    for load in loads:
        load.start()
    cycles = coeff_out.shape[0]
    groups = coeff_out.shape[1]
    slots = alm.shape[0] // (2 * fields)

    def any_peer(i):
        other = lax.rem(mine + i, everyone)
        return {"half": other // devs, "dev": lax.rem(other, devs)}

    ready = meet(everyone, any_peer)
    for load in loads:
        load.wait()
    full = lax.dot_general(legendre[...], alm[...], SIDES, preferred_element_type=jnp.float32)
    lane = lax.broadcasted_iota(jnp.int32, (cycles, full.shape[1]), 1) // (2 * fields)
    own = jnp.zeros((cycles, full.shape[1]), jnp.float32)
    for s in range(slots):
        own = jnp.where(lane == s, full[s * cycles : (s + 1) * cycles], own)
    for q in range(groups):
        coeff_out[:, q, :] = own[:, q * TILE : (q + 1) * TILE]
    ready()

    def coeff_copy(target_half, target_dev, from_half, from_dev, n_out, n_in):
        return pltpu.make_async_remote_copy(
            src_ref=coeff_out.at[target_dev],
            dst_ref=coeff_in.at[from_half, from_dev],
            send_sem=sent.at[n_out],
            recv_sem=got.at[n_in],
            device_id={"half": target_half, "dev": target_dev},
            device_id_type=MESH,
        )

    def send_coeff(i, carry):
        other = lax.rem(mine + i, everyone)
        coeff_copy(other // devs, lax.rem(other, devs), half, dev, other, mine).start()
        return carry

    lax.fori_loop(1, everyone, send_coeff, 0)
    coeff_in[half, dev] = coeff_out[dev]

    total = orders.shape[1]
    per_group = slots // groups
    place = lax.broadcasted_iota(jnp.int32, (total, total), 1)
    place = place % devs * slots + place // devs % groups * per_group + place // (devs * groups)
    moves = (lax.broadcasted_iota(jnp.int32, (total, total), 0) == place).astype(jnp.float32)
    ids = jnp.dot(
        orders[...].astype(jnp.float32), moves, precision=HIGHEST,
        preferred_element_type=jnp.float32,
    )
    ids = jnp.round(ids).astype(jnp.int32)
    per_cycle = NPHI // TILE
    weight = jnp.where(ids == 0, 1.0, 2.0) / math.sqrt(2.0 * total)
    outer = lax.broadcasted_iota(jnp.int32, (per_cycle, total), 0) * (2 * TILE)
    inner = lax.broadcasted_iota(jnp.int32, (TILE, total), 0) * 2 + 1
    cos_out, sin_out = cos_sin(outer * ids % (2 * NPHI))
    basis = jnp.concatenate(cos_sin(inner * ids % (2 * NPHI)), axis=1)
    spread = []
    row_field = lax.broadcasted_iota(jnp.int32, (2 * fields, fields), 0) % fields
    pick_row = row_field == lax.broadcasted_iota(jnp.int32, (2 * fields, fields), 1)
    wide = (2 * fields, TILE)
    same = lax.broadcasted_iota(jnp.int32, wide, 0) // fields == (
        lax.broadcasted_iota(jnp.int32, wide, 1) // fields
    ) % 2
    for h in range(halves):
        lanes = (mix.shape[1], TILE)
        pick_lane = lax.broadcasted_iota(jnp.int32, lanes, 0) == (
            lax.broadcasted_iota(jnp.int32, lanes, 1) % fields + h * fields
        )
        rows = jnp.dot(
            pick_row.astype(jnp.float32), mix[...], precision=HIGHEST,
            preferred_element_type=jnp.float32,
        )
        rows = jnp.dot(
            rows, pick_lane.astype(jnp.float32), precision=HIGHEST,
            preferred_element_type=jnp.float32,
        )
        spread.append(jnp.where(same, rows, 0.0))

    def wait_coeff(i, carry):
        other = lax.rem(mine + i, everyone)
        copy = coeff_copy(
            other // devs, lax.rem(other, devs), other // devs, lax.rem(other, devs), other, other
        )
        copy.wait_recv()
        copy.wait_send()
        return carry

    scan_count, block_total = block_tile.shape
    length = pix.shape[1]
    block_len = length // block_total
    lags = noise.shape[1]
    per_block = block_len // COLS
    halo = lags // COLS
    window = 2 * lags + COLS
    rows = (length // COLS) * fields
    padded = (even, odd)
    edge = jnp.zeros((halo * fields, COLS), jnp.bfloat16)
    for ref in padded:
        ref[: halo * fields, :] = edge
        ref[halo * fields + rows :, :] = edge
    taps = noise[...].astype(jnp.bfloat16).astype(jnp.float32)
    lane = lax.broadcasted_iota(jnp.int32, taps.shape, 1)
    moved = jnp.where(lane == lags - 1, 0.0, pltpu.roll(taps, lags - 1, 1))
    turn = (
        lax.broadcasted_iota(jnp.int32, (TILE, TILE), 0)
        + lax.broadcasted_iota(jnp.int32, (TILE, TILE), 1)
        == TILE - 1
    ).astype(jnp.float32).astype(jnp.bfloat16)
    chunks = lags // TILE
    blank = jnp.zeros((scan_count, TILE), jnp.float32)
    turned = [
        jnp.dot(
            moved[:, c * TILE : (c + 1) * TILE].astype(jnp.bfloat16),
            turn,
            preferred_element_type=jnp.float32,
        )
        for c in range(chunks)
    ]
    band = jnp.concatenate([blank] + turned[::-1] + [taps] + [blank] * 2, axis=1)
    width = band.shape[1]
    top = width - COLS
    for n in range(scan_count):
        strip = pltpu.roll(
            jnp.broadcast_to(band[n : n + 1], (TILE, width)), 0, 1, stride=1, stride_axis=0
        ).astype(jnp.bfloat16)
        for q in range(window // TILE):
            start = top - q * TILE
            table[n, q * TILE : (q + 1) * TILE, :] = strip[:, start : start + COLS]

    lax.fori_loop(1, everyone, wait_coeff, 0)
    coeff = jnp.zeros((2 * fields, total), jnp.float32)
    for h in range(halves):
        block = jnp.concatenate([coeff_in[h, :, q, :] for q in range(groups)], axis=0)
        group = lax.broadcasted_iota(jnp.int32, block.shape, 1) // (2 * fields)
        block = jnp.concatenate(
            [jnp.where(group == s, block, 0.0) for s in range(per_group)], axis=0
        )
        coeff = coeff + lax.dot_general(
            spread[h], block, SIDES, precision=HIGHEST, preferred_element_type=jnp.float32
        )
    coeff = coeff * weight
    real, imag = coeff[:fields], coeff[fields:]
    turned = []
    for a in range(per_cycle):
        c, s = cos_out[a : a + 1], sin_out[a : a + 1]
        turned.append(jnp.concatenate([real * c - imag * s, -(real * s + imag * c)], axis=1))
    pixels = lax.dot_general(
        jnp.concatenate(turned, axis=0), basis, SIDES, precision=HIGHEST,
        preferred_element_type=jnp.float32,
    ).astype(jnp.bfloat16)
    for a in range(per_cycle):
        tiles[a] = pixels[a * fields : (a + 1) * fields]

    def tile_copy(target, source):
        return pltpu.make_async_remote_copy(
            src_ref=tiles_out.at[target],
            dst_ref=tiles_in.at[source],
            send_sem=tile_sent.at[target],
            recv_sem=tile_got.at[source],
            device_id={"half": half, "dev": target},
            device_id_type=MESH,
        )

    def send_tiles(i, carry):
        other = lax.rem(dev + i, devs)
        for k in range(caps):
            tiles_out[other, k] = tiles[jnp.maximum(owner[dev, k, other], 0)]
        tile_copy(other, dev).start()
        return carry

    lax.fori_loop(1, devs, send_tiles, 0)
    for k in range(caps):
        tiles_in[dev, k] = tiles[jnp.maximum(owner[dev, k, dev], 0)]

    def wait_tiles(i, carry):
        other = lax.rem(dev + i, devs)
        pltpu.make_async_remote_copy(
            src_ref=tiles_out.at[other],
            dst_ref=tiles_in.at[other],
            send_sem=tile_sent.at[other],
            recv_sem=tile_got.at[other],
            device_id={"half": half, "dev": other},
            device_id_type=MESH,
        ).wait()
        return carry

    slot_total = devs * caps
    select_shape = (slot_total, scan_count * block_total)
    slot_iota = lax.broadcasted_iota(jnp.int32, select_shape, 0)
    block_iota = lax.broadcasted_iota(jnp.int32, select_shape, 1)

    def mark(i, select):
        n, b = i // block_total, i % block_total
        slot = scan_tiles[n, block_tile[n, b]]
        return jnp.where((slot_iota == slot) & (block_iota == i), 1.0, select)

    select = lax.fori_loop(
        0, scan_count * block_total, mark, jnp.zeros(select_shape, jnp.float32)
    ).astype(jnp.bfloat16)
    lax.fori_loop(1, devs, wait_tiles, 0)


    below = lax.broadcasted_iota(jnp.int32, (TILE, block_len), 0).astype(jnp.float32).astype(
        jnp.bfloat16
    )

    def sample(n, b):
        slot = scan_tiles[n, block_tile[n, b]]
        tile = tiles_in[slot // caps, slot % caps].astype(jnp.float32)
        for c in range(block_len // TILE):
            at = pl.multiple_of(b * block_len + c * TILE, TILE)
            index = jnp.broadcast_to(pix[n : n + 1, pl.ds(at, TILE)], tile.shape)
            value = jnp.take_along_axis(
                tile, jnp.maximum(index, 0), axis=1, mode="promise_in_bounds"
            )
            value = jnp.where(index >= 0, value, 0.0).astype(jnp.bfloat16)
            row = pl.multiple_of((b * per_block + (c * TILE) // COLS + halo) * fields, 16)
            lane_at = (c * TILE) % COLS
            padded[n % 2][pl.ds(row, fields), lane_at : lane_at + TILE] = value

    def collect(n, b):
        at = pl.multiple_of(b * block_len, TILE)
        index = pix[n : n + 1, pl.ds(at, block_len)].astype(jnp.float32).astype(jnp.bfloat16)
        hot = jnp.where(
            below == index, jnp.ones((), jnp.bfloat16), jnp.zeros((), jnp.bfloat16)
        )
        row = jnp.concatenate(
            [
                weighted[pl.ds(pl.multiple_of((b * per_block + i) * fields, 16), fields), :]
                for i in range(per_block)
            ],
            axis=1,
        )
        part = lax.dot_general(
            row, hot, (((1,), (1,)), ((), ())), preferred_element_type=jnp.float32
        )
        parts[n * block_total + b] = part

    def together(step, group):
        def body(m, carry):
            for k in range(group):
                step(m * group + k)
            return carry

        lax.fori_loop(0, block_total // group, body, 0)

    group = 4
    while block_total % group:
        group //= 2
    together(lambda b: sample(0, b), group)
    for n in range(scan_count):
        pieces = [
            padded[n % 2][o * fields : o * fields + rows, :] for o in range(2 * halo + 1)
        ]
        filtered = jnp.dot(
            jnp.concatenate(pieces, axis=1), table[n], preferred_element_type=jnp.float32
        )
        weighted[...] = (scan_weight[n] * filtered).astype(jnp.bfloat16)

        def step(b):
            collect(n, b)
            if n + 1 < scan_count:
                sample(n + 1, b)

        together(step, group)
    for f in range(fields):
        exact = parts[:, f, :]
        high = exact.astype(jnp.bfloat16)
        low = (exact - high.astype(jnp.float32)).astype(jnp.bfloat16)
        sums[:, f, :] = jnp.dot(select, high, preferred_element_type=jnp.float32) + jnp.dot(
            select, low, preferred_element_type=jnp.float32
        )
    for e in range(devs):
        for k in range(caps):
            back_out[e, k] = sums[e * caps + k].astype(back_out.dtype)

    def back_copy(target, source):
        return pltpu.make_async_remote_copy(
            src_ref=back_out.at[target],
            dst_ref=back_in.at[source],
            send_sem=back_sent.at[target],
            recv_sem=back_got.at[source],
            device_id={"half": half, "dev": target},
            device_id_type=MESH,
        )

    def send_back(i, carry):
        back_copy(lax.rem(dev + i, devs), dev).start()
        return carry

    lax.fori_loop(1, devs, send_back, 0)
    back_in[dev] = back_out[dev]

    def wait_back(i, carry):
        other = lax.rem(dev + i, devs)
        back_copy(other, other).wait()
        return carry

    lax.fori_loop(1, devs, wait_back, 0)
    out[...] = back_in[...]


def whole_part(
    owner, scan_tiles, block_tile, scan_weight, orders, field_mix, alm, legendre, pix, noise, devs,
    halves,
):
    caps = owner.shape[1]
    fields = field_mix.shape[0]
    groups = alm.shape[0] // TILE
    cycles = legendre.shape[0] * 2 * fields // alm.shape[0]
    scan_count, lags = noise.shape
    length = pix.shape[1]
    blocks = scan_count * block_tile.shape[1]
    exchanged = (devs, caps, fields, TILE)
    halo_rows = (length + 2 * lags) // COLS * fields
    loads = (orders, field_mix, alm, legendre, pix, noise)
    return pl.pallas_call(
        whole_kernel,
        out_shape=jax.ShapeDtypeStruct(exchanged, jnp.bfloat16),
        in_specs=[pl.BlockSpec(memory_space=SMEM)] * 4
        + [pl.BlockSpec(memory_space=pltpu.HBM)] * len(loads),
        out_specs=pl.BlockSpec(memory_space=VMEM),
        scratch_shapes=[VMEM(x.shape, x.dtype) for x in loads]
        + [
            VMEM((cycles, groups, TILE), jnp.float32),
            VMEM((halves, devs, groups, TILE), jnp.float32),
            VMEM((NPHI // TILE, fields, TILE), jnp.bfloat16),
            VMEM(exchanged, jnp.bfloat16),
            VMEM(exchanged, jnp.bfloat16),
            VMEM((scan_count, 2 * lags + COLS, COLS), jnp.bfloat16),
            VMEM((halo_rows, COLS), jnp.bfloat16),
            VMEM((halo_rows, COLS), jnp.bfloat16),
            VMEM((length // COLS * fields, COLS), jnp.bfloat16),
            VMEM((blocks, fields, TILE), jnp.float32),
            VMEM((devs * caps, fields, TILE), jnp.float32),
            VMEM(exchanged, jnp.bfloat16),
            VMEM(exchanged, jnp.bfloat16),
            pltpu.SemaphoreType.DMA((len(loads),)),
            pltpu.SemaphoreType.DMA((halves * devs,)),
            pltpu.SemaphoreType.DMA((halves * devs,)),
            pltpu.SemaphoreType.DMA((devs,)),
            pltpu.SemaphoreType.DMA((devs,)),
            pltpu.SemaphoreType.DMA((devs,)),
            pltpu.SemaphoreType.DMA((devs,)),
        ],
        compiler_params=pltpu.CompilerParams(
            collective_id=0, has_side_effects=True, vmem_limit_bytes=60 * 2**20
        ),
        name="whole",
    )(owner, scan_tiles, block_tile, scan_weight, *loads)


def place_kernel(owner, parts, out):
    caps = owner.shape[1]
    dev = lax.axis_index("dev")
    out[...] = jnp.zeros(out.shape, out.dtype)

    def one(e, carry):
        for k in range(caps):
            tile = owner[dev, k, e]
            at = pl.ds(pl.multiple_of(jnp.maximum(tile, 0) * TILE, TILE), TILE)
            out[0, :, at] += jnp.where(tile >= 0, parts[e, k].astype(out.dtype), 0.0)
        return carry

    lax.fori_loop(0, owner.shape[2], one, 0)


def place_part(owner, parts):
    return pl.pallas_call(
        place_kernel,
        out_shape=jax.ShapeDtypeStruct((1, parts.shape[2], NPHI), jnp.float32),
        in_specs=[pl.BlockSpec(memory_space=SMEM), pl.BlockSpec(memory_space=VMEM)],
        out_specs=pl.BlockSpec(memory_space=VMEM),
        compiler_params=pltpu.CompilerParams(vmem_limit_bytes=32 * 2**20),
        name="placing",
    )(owner, parts)


def local(
    field_mix,
    alm,
    legendre,
    order_ids,
    fetch_list,
    scan_tiles,
    block_tile,
    block_pix,
    noise_kernel,
    scan_weight,
):
    devs = lax.axis_size("dev")
    halves = lax.axis_size("half")
    order_slots, parts, fields, ells = alm.shape
    cycles = legendre.shape[2]
    owner = fetch_list.transpose(0, 2, 1)
    returned = whole_part(
        owner,
        scan_tiles,
        block_tile,
        scan_weight,
        order_ids.reshape(1, -1),
        field_mix,
        alm.reshape(order_slots * parts * fields, ells),
        legendre.transpose(0, 2, 1).reshape(order_slots * cycles, ells),
        block_pix,
        noise_kernel,
        devs,
        halves,
    )
    return place_part(owner, returned)


def solution(mesh):
    return jax.shard_map(
        local,
        mesh=mesh,
        in_specs=(
            P("half", None),
            P("dev", None, "half", None),
            P("dev", None, None),
            P(),
            P(),
            P("dev", None),
            P("dev", None),
            P("dev", None),
            P("dev", None),
            P("dev"),
        ),
        out_specs=P("dev", "half", None),
        check_vma=False,
    )
```

time: 48 us -> 44.4 us (0.925)
  local copies, waits for them, and re-layouts: 4.96 us -> 0.9 us
  Pallas kernels: 42.6 us -> 43.3 us
    unnamed x20 -> x4, local copies, waits for them, and re-layouts: 4.96 us -> 0.9 us
    pallas_call x3 -> x1, Pallas kernels: 40.8 us -> 41.5 us  [whole_part(): pl.pallas_call(whole_kernel, out_shape=jax.ShapeDtypeStruct(exchanged, jn...]
where the time goes in v4:
time: 44.4 us; the launch traced here: 44.2 us
  Pallas kernels  43.3 us (98%)
  local copies, waits for them, and re-layouts  0.9 us (2%)
    pallas_call x1, Pallas kernels, whole_part(): pl.pallas_call(whole_kernel, out_shape=jax.ShapeDtypeStruct(exchanged, jn...  41.5 us
    pallas_call x1, Pallas kernels, place_part(): pl.pallas_call(place_kernel, out_shape=jax.ShapeDtypeStruct((1, parts.sha...  1.78 us
    unnamed x4, local copies, waits for them, and re-layouts  0.9 us

profile of v4, /device:TPU:0, one launch (start us, length us, event | category | flops | bytes accessed | tf_op | source)
XLA Modules:
  0.0 44.2 jit_solution(10714608105372948949)
XLA Ops:
  0.0 0.0 copy-start.1
  0.0 41.5 %whole.1.parts = bf16[16,2,16,128]{3,2,1,0:T(8,128)(2,1)} custom-call(s32[16,2,16]{2,1,0:T(2,128)} %bitcast.6, s32[4,32]{1,0:T(4,128)} %scan_tiles.1, s32[4,32]{1,0:T(4,128)} %block_tile.1, f32[4]{0:T(128)} %scan_weight.1, s32[1,128]{1,0:T(1,128)} %bitcast.10, f32[16,32]{1,0:T(8,128)} %mix_hbm.1, bf16[256,2048]{1,0:T(8,128)(2,1)} %bitcast.8, ...), custom_call_target="tpu_custom_call" | custom-call | tf_op jit(solution)/shard_map/whole/pallas_call | solution.py:388
  41.5 0.0 copy-done.1
  41.5 0.0 copy-start
  41.5 0.9 %copy-done = bf16[16,2,16,128]{3,2,1,0:T(8,128)(2,1)S(1)} copy-done((bf16[16,2,16,128]{3,2,1,0:T(8,128)(2,1)S(1)}, bf16[16,2,16,128]{3,2,1,0:T(8,128)(2,1)}, u32[]{:S(2)}) %copy-start) | copy-done | bytes 131096
  42.4 1.8 %placing.1 = f32[1,16,4096]{2,1,0:T(8,128)} custom-call(s32[16,2,16]{2,1,0:T(2,128)S(1)} %bitcast.7, bf16[16,2,16,128]{3,2,1,0:T(8,128)(2,1)S(1)} %copy-done), custom_call_target="tpu_custom_call" | custom-call | tf_op jit(solution)/shard_map/placing/pallas_call | solution.py:440
Async XLA Ops:
  0.0 41.5 %copy-start.1 = (s32[16,16,2]{1,2,0:T(2,128)S(1)}, s32[16,16,2]{1,2,0:T(2,128)}, u32[]{:S(2)}) copy-start(s32[16,16,2]{1,2,0:T(2,128)} %param.14) | copy-start | bytes 6148
  41.5 0.9 %copy-start = (bf16[16,2,16,128]{3,2,1,0:T(8,128)(2,1)S(1)}, bf16[16,2,16,128]{3,2,1,0:T(8,128)(2,1)}, u32[]{:S(2)}) copy-start(bf16[16,2,16,128]{3,2,1,0:T(8,128)(2,1)} %whole.1.parts) | copy-start | bytes 393220

commit v5 on v4

--- a/solution.py
+++ b/solution.py
@@ -47,8 +47,8 @@
 def whole_kernel(
     owner, scan_tiles, block_tile, scan_weight, orders_hbm, mix_hbm, alm_hbm, legendre_hbm,
     pix_hbm, noise_hbm, out, orders, mix, alm, legendre, pix, noise, coeff_out, coeff_in, tiles,
-    tiles_out, tiles_in, table, even, odd, weighted, parts, sums, back_out, back_in, loaded, sent,
-    got, tile_sent, tile_got, back_sent, back_got,
+    tiles_out, tiles_in, table, points, padded, weighted, parts, sums, own_tiles, back_out,
+    back_in, loaded, sent, got, tile_sent, tile_got, back_sent, back_got,
 ):
     half, dev = lax.axis_index("half"), lax.axis_index("dev")
     halves, devs = lax.axis_size("half"), lax.axis_size("dev")
@@ -164,11 +164,17 @@
     halo = lags // COLS
     window = 2 * lags + COLS
     rows = (length // COLS) * fields
-    padded = (even, odd)
     edge = jnp.zeros((halo * fields, COLS), jnp.bfloat16)
-    for ref in padded:
-        ref[: halo * fields, :] = edge
-        ref[halo * fields + rows :, :] = edge
+    padded[: halo * fields, :] = edge
+    padded[halo * fields + rows :, :] = edge
+    for n in range(scan_count):
+
+        def cut(b, carry):
+            at = pl.multiple_of(b * block_len, TILE)
+            points[n * block_total + b] = pix[n : n + 1, pl.ds(at, block_len)]
+            return carry
+
+        lax.fori_loop(0, block_total, cut, 0, unroll=4)
     taps = noise[...].astype(jnp.bfloat16).astype(jnp.float32)
     lane = lax.broadcasted_iota(jnp.int32, taps.shape, 1)
     moved = jnp.where(lane == lags - 1, 0.0, pltpu.roll(taps, lags - 1, 1))
@@ -268,6 +274,17 @@
     select = lax.fori_loop(
         0, scan_count * block_total, mark, jnp.zeros(select_shape, jnp.float32)
     ).astype(jnp.bfloat16)
+    place_shape = (per_cycle, slot_total)
+    tile_iota = lax.broadcasted_iota(jnp.int32, place_shape, 0)
+    place_iota = lax.broadcasted_iota(jnp.int32, place_shape, 1)
+
+    def mark_tile(i, placing):
+        tile = owner[dev, i % caps, i // caps]
+        return jnp.where((tile_iota == tile) & (place_iota == i), 1.0, placing)
+
+    placing = lax.fori_loop(
+        0, slot_total, mark_tile, jnp.zeros(place_shape, jnp.float32)
+    ).astype(jnp.bfloat16)
     lax.fori_loop(1, devs, wait_tiles, 0)
 
 
@@ -279,19 +296,18 @@
         slot = scan_tiles[n, block_tile[n, b]]
         tile = tiles_in[slot // caps, slot % caps].astype(jnp.float32)
         for c in range(block_len // TILE):
-            at = pl.multiple_of(b * block_len + c * TILE, TILE)
-            index = jnp.broadcast_to(pix[n : n + 1, pl.ds(at, TILE)], tile.shape)
+            index = points[n * block_total + b, :, c * TILE : (c + 1) * TILE]
+            index = jnp.broadcast_to(index, tile.shape)
             value = jnp.take_along_axis(
                 tile, jnp.maximum(index, 0), axis=1, mode="promise_in_bounds"
             )
             value = jnp.where(index >= 0, value, 0.0).astype(jnp.bfloat16)
             row = pl.multiple_of((b * per_block + (c * TILE) // COLS + halo) * fields, 16)
             lane_at = (c * TILE) % COLS
-            padded[n % 2][pl.ds(row, fields), lane_at : lane_at + TILE] = value
+            padded[pl.ds(row, fields), lane_at : lane_at + TILE] = value
 
     def collect(n, b):
-        at = pl.multiple_of(b * block_len, TILE)
-        index = pix[n : n + 1, pl.ds(at, block_len)].astype(jnp.float32).astype(jnp.bfloat16)
+        index = points[n * block_total + b].astype(jnp.float32).astype(jnp.bfloat16)
         hot = jnp.where(
             below == index, jnp.ones((), jnp.bfloat16), jnp.zeros((), jnp.bfloat16)
         )
@@ -315,14 +331,13 @@
 
         lax.fori_loop(0, block_total // group, body, 0)
 
-    group = 4
+    group = 16
     while block_total % group:
         group //= 2
     together(lambda b: sample(0, b), group)
-    for n in range(scan_count):
-        pieces = [
-            padded[n % 2][o * fields : o * fields + rows, :] for o in range(2 * halo + 1)
-        ]
+
+    def one_scan(n, carry):
+        pieces = [padded[o * fields : o * fields + rows, :] for o in range(2 * halo + 1)]
         filtered = jnp.dot(
             jnp.concatenate(pieces, axis=1), table[n], preferred_element_type=jnp.float32
         )
@@ -330,10 +345,12 @@
 
         def step(b):
             collect(n, b)
-            if n + 1 < scan_count:
-                sample(n + 1, b)
+            sample(lax.min(n + 1, scan_count - 1), b)
 
         together(step, group)
+        return carry
+
+    lax.fori_loop(0, scan_count, one_scan, 0)
     for f in range(fields):
         exact = parts[:, f, :]
         high = exact.astype(jnp.bfloat16)
@@ -368,7 +385,15 @@
         return carry
 
     lax.fori_loop(1, devs, wait_back, 0)
-    out[...] = back_in[...]
+    for e in range(devs):
+        for k in range(caps):
+            sums[e * caps + k] = back_in[e, k].astype(jnp.float32)
+    for f in range(fields):
+        own_tiles[:, f, :] = jnp.dot(
+            placing, sums[:, f, :].astype(jnp.bfloat16), preferred_element_type=jnp.float32
+        )
+    for a in range(per_cycle):
+        out[0, :, a * TILE : (a + 1) * TILE] = own_tiles[a]
 
 
 def whole_part(
@@ -387,7 +412,7 @@
     loads = (orders, field_mix, alm, legendre, pix, noise)
     return pl.pallas_call(
         whole_kernel,
-        out_shape=jax.ShapeDtypeStruct(exchanged, jnp.bfloat16),
+        out_shape=jax.ShapeDtypeStruct((1, fields, NPHI), jnp.float32),
         in_specs=[pl.BlockSpec(memory_space=SMEM)] * 4
         + [pl.BlockSpec(memory_space=pltpu.HBM)] * len(loads),
         out_specs=pl.BlockSpec(memory_space=VMEM),
@@ -399,11 +424,12 @@
             VMEM(exchanged, jnp.bfloat16),
             VMEM(exchanged, jnp.bfloat16),
             VMEM((scan_count, 2 * lags + COLS, COLS), jnp.bfloat16),
-            VMEM((halo_rows, COLS), jnp.bfloat16),
+            VMEM((blocks, 1, length // block_tile.shape[1]), jnp.int32),
             VMEM((halo_rows, COLS), jnp.bfloat16),
             VMEM((length // COLS * fields, COLS), jnp.bfloat16),
             VMEM((blocks, fields, TILE), jnp.float32),
             VMEM((devs * caps, fields, TILE), jnp.float32),
+            VMEM((NPHI // TILE, fields, TILE), jnp.float32),
             VMEM(exchanged, jnp.bfloat16),
             VMEM(exchanged, jnp.bfloat16),
             pltpu.SemaphoreType.DMA((len(loads),)),
@@ -419,32 +445,6 @@
         ),
         name="whole",
     )(owner, scan_tiles, block_tile, scan_weight, *loads)
-
-
-def place_kernel(owner, parts, out):
-    caps = owner.shape[1]
-    dev = lax.axis_index("dev")
-    out[...] = jnp.zeros(out.shape, out.dtype)
-
-    def one(e, carry):
-        for k in range(caps):
-            tile = owner[dev, k, e]
-            at = pl.ds(pl.multiple_of(jnp.maximum(tile, 0) * TILE, TILE), TILE)
-            out[0, :, at] += jnp.where(tile >= 0, parts[e, k].astype(out.dtype), 0.0)
-        return carry
-
-    lax.fori_loop(0, owner.shape[2], one, 0)
-
-
-def place_part(owner, parts):
-    return pl.pallas_call(
-        place_kernel,
-        out_shape=jax.ShapeDtypeStruct((1, parts.shape[2], NPHI), jnp.float32),
-        in_specs=[pl.BlockSpec(memory_space=SMEM), pl.BlockSpec(memory_space=VMEM)],
-        out_specs=pl.BlockSpec(memory_space=VMEM),
-        compiler_params=pltpu.CompilerParams(vmem_limit_bytes=32 * 2**20),
-        name="placing",
-    )(owner, parts)
 
 
 def local(
@@ -464,7 +464,7 @@
     order_slots, parts, fields, ells = alm.shape
     cycles = legendre.shape[2]
     owner = fetch_list.transpose(0, 2, 1)
-    returned = whole_part(
+    return whole_part(
         owner,
         scan_tiles,
         block_tile,
@@ -478,7 +478,6 @@
         devs,
         halves,
     )
-    return place_part(owner, returned)
 
 
 def solution(mesh):

time: 44.4 us -> 39.9 us (0.90)
  Pallas kernels: 43.3 us -> 38 us
  local copies, waits for them, and re-layouts: 0.9 us -> 1.67 us
    pallas_call x2 -> x1, Pallas kernels: 43.3 us -> 38 us  [whole_part(): pl.pallas_call(whole_kernel, out_shape=jax.ShapeDtypeStruct((1, fields, N...]
    unnamed x4 -> x1, local copies, waits for them, and re-layouts: 0.9 us -> 1.67 us
where the time goes in v5:
time: 39.9 us; the launch traced here: 39.6 us
  Pallas kernels  38 us (95%)
  local copies, waits for them, and re-layouts  1.67 us (4%)
    pallas_call x1, Pallas kernels, whole_part(): pl.pallas_call(whole_kernel, out_shape=jax.ShapeDtypeStruct((1, fields, N...  38 us
    unnamed x1, local copies, waits for them, and re-layouts  1.67 us

profile of v5, /device:TPU:0, one launch (start us, length us, event | category | flops | bytes accessed | tf_op | source)
XLA Modules:
  0.0 39.6 jit_solution(609543550799184181)
XLA Ops:
  0.0 38.0 %whole.1 = f32[1,16,4096]{2,1,0:T(8,128)} custom-call(s32[16,2,16]{2,1,0:T(2,128)} %bitcast.8, s32[4,32]{1,0:T(4,128)} %scan_tiles.1, s32[4,32]{1,0:T(4,128)} %block_tile.1, f32[4]{0:T(128)} %scan_weight.1, s32[1,128]{1,0:T(1,128)} %bitcast.9, f32[16,32]{1,0:T(8,128)} %mix_hbm.1, bf16[256,2048]{1,0:T(8,128)(2,1)} %bitcast.6, bf16[128,2048]{1,0:T(8,128)(2,1)} %bitcast.7, ...), custom_call_target="tpu_custom_call" | custom-call | tf_op jit(solution)/shard_map/whole/pallas_call | solution.py:413
  38.0 1.7 %copy.12 = f32[1,16,4096]{2,1,0:T(8,128)} copy(f32[1,16,4096]{2,1,0:T(8,128)} %whole.1) | data formatting | bytes 524288

commit v6 on v5

--- a/solution.py
+++ b/solution.py
@@ -11,6 +11,7 @@
 NPHI = 4096
 TILE = 128
 COLS = 256
+ROWS = 8
 VMEM = pltpu.VMEM
 SMEM = pltpu.SMEM
 
@@ -47,7 +48,7 @@
 def whole_kernel(
     owner, scan_tiles, block_tile, scan_weight, orders_hbm, mix_hbm, alm_hbm, legendre_hbm,
     pix_hbm, noise_hbm, out, orders, mix, alm, legendre, pix, noise, coeff_out, coeff_in, tiles,
-    tiles_out, tiles_in, table, points, padded, weighted, parts, sums, own_tiles, back_out,
+    tiles_out, tiles_in, table, points, padded, weighted, parts, sums, back_out,
     back_in, loaded, sent, got, tile_sent, tile_got, back_sent, back_got,
 ):
     half, dev = lax.axis_index("half"), lax.axis_index("dev")
@@ -120,7 +121,7 @@
     )
     ids = jnp.round(ids).astype(jnp.int32)
     per_cycle = NPHI // TILE
-    weight = jnp.where(ids == 0, 1.0, 2.0) / math.sqrt(2.0 * total)
+    weight = jnp.where(ids == 0, 1.0, 2.0)
     outer = lax.broadcasted_iota(jnp.int32, (per_cycle, total), 0) * (2 * TILE)
     inner = lax.broadcasted_iota(jnp.int32, (TILE, total), 0) * 2 + 1
     cos_out, sin_out = cos_sin(outer * ids % (2 * NPHI))
@@ -149,11 +150,8 @@
 
     def wait_coeff(i, carry):
         other = lax.rem(mine + i, everyone)
-        copy = coeff_copy(
-            other // devs, lax.rem(other, devs), other // devs, lax.rem(other, devs), other, other
-        )
-        copy.wait_recv()
-        copy.wait_send()
+        there, at = other // devs, lax.rem(other, devs)
+        coeff_copy(there, at, there, at, other, other).wait_recv()
         return carry
 
     scan_count, block_total = block_tile.shape
@@ -164,9 +162,6 @@
     halo = lags // COLS
     window = 2 * lags + COLS
     rows = (length // COLS) * fields
-    edge = jnp.zeros((halo * fields, COLS), jnp.bfloat16)
-    padded[: halo * fields, :] = edge
-    padded[halo * fields + rows :, :] = edge
     for n in range(scan_count):
 
         def cut(b, carry):
@@ -175,6 +170,59 @@
             return carry
 
         lax.fori_loop(0, block_total, cut, 0, unroll=4)
+    lax.fori_loop(1, everyone, wait_coeff, 0)
+    coeff = jnp.zeros((2 * fields, total), jnp.float32)
+    for h in range(halves):
+        block = jnp.concatenate([coeff_in[h, :, q, :] for q in range(groups)], axis=0)
+        group = lax.broadcasted_iota(jnp.int32, block.shape, 1) // (2 * fields)
+        block = jnp.concatenate(
+            [jnp.where(group == s, block, 0.0) for s in range(per_group)], axis=0
+        )
+        coeff = coeff + lax.dot_general(
+            spread[h], block, SIDES, precision=HIGHEST, preferred_element_type=jnp.float32
+        )
+    coeff = coeff * weight
+    real, imag = coeff[:fields], coeff[fields:]
+    turned = []
+    for a in range(per_cycle):
+        c, s = cos_out[a : a + 1], sin_out[a : a + 1]
+        turned.append(jnp.concatenate([real * c - imag * s, -(real * s + imag * c)], axis=1))
+    pixels = lax.dot_general(
+        jnp.concatenate(turned, axis=0), basis, SIDES, precision=HIGHEST,
+        preferred_element_type=jnp.float32,
+    ).astype(jnp.bfloat16)
+    for a in range(per_cycle):
+        tiles[a] = pixels[a * fields : (a + 1) * fields]
+
+    def tile_copy(target, source):
+        return pltpu.make_async_remote_copy(
+            src_ref=tiles_out.at[target],
+            dst_ref=tiles_in.at[source],
+            send_sem=tile_sent.at[target],
+            recv_sem=tile_got.at[source],
+            device_id={"half": half, "dev": target},
+            device_id_type=MESH,
+        )
+
+    def send_tiles(i, carry):
+        other = lax.rem(dev + i, devs)
+        for k in range(caps):
+            tiles_out[other, k] = tiles[jnp.maximum(owner[dev, k, other], 0)]
+        tile_copy(other, dev).start()
+        return carry
+
+    lax.fori_loop(1, devs, send_tiles, 0)
+    for k in range(caps):
+        tiles_in[dev, k] = tiles[jnp.maximum(owner[dev, k, dev], 0)]
+
+    def wait_tiles(i, carry):
+        other = lax.rem(dev + i, devs)
+        tile_copy(other, other).wait_recv()
+        return carry
+
+    edge = jnp.zeros((halo * fields, COLS), jnp.bfloat16)
+    padded[: halo * fields, :] = edge
+    padded[halo * fields + rows :, :] = edge
     taps = noise[...].astype(jnp.bfloat16).astype(jnp.float32)
     lane = lax.broadcasted_iota(jnp.int32, taps.shape, 1)
     moved = jnp.where(lane == lags - 1, 0.0, pltpu.roll(taps, lags - 1, 1))
@@ -204,63 +252,6 @@
             start = top - q * TILE
             table[n, q * TILE : (q + 1) * TILE, :] = strip[:, start : start + COLS]
 
-    lax.fori_loop(1, everyone, wait_coeff, 0)
-    coeff = jnp.zeros((2 * fields, total), jnp.float32)
-    for h in range(halves):
-        block = jnp.concatenate([coeff_in[h, :, q, :] for q in range(groups)], axis=0)
-        group = lax.broadcasted_iota(jnp.int32, block.shape, 1) // (2 * fields)
-        block = jnp.concatenate(
-            [jnp.where(group == s, block, 0.0) for s in range(per_group)], axis=0
-        )
-        coeff = coeff + lax.dot_general(
-            spread[h], block, SIDES, precision=HIGHEST, preferred_element_type=jnp.float32
-        )
-    coeff = coeff * weight
-    real, imag = coeff[:fields], coeff[fields:]
-    turned = []
-    for a in range(per_cycle):
-        c, s = cos_out[a : a + 1], sin_out[a : a + 1]
-        turned.append(jnp.concatenate([real * c - imag * s, -(real * s + imag * c)], axis=1))
-    pixels = lax.dot_general(
-        jnp.concatenate(turned, axis=0), basis, SIDES, precision=HIGHEST,
-        preferred_element_type=jnp.float32,
-    ).astype(jnp.bfloat16)
-    for a in range(per_cycle):
-        tiles[a] = pixels[a * fields : (a + 1) * fields]
-
-    def tile_copy(target, source):
-        return pltpu.make_async_remote_copy(
-            src_ref=tiles_out.at[target],
-            dst_ref=tiles_in.at[source],
-            send_sem=tile_sent.at[target],
-            recv_sem=tile_got.at[source],
-            device_id={"half": half, "dev": target},
-            device_id_type=MESH,
-        )
-
-    def send_tiles(i, carry):
-        other = lax.rem(dev + i, devs)
-        for k in range(caps):
-            tiles_out[other, k] = tiles[jnp.maximum(owner[dev, k, other], 0)]
-        tile_copy(other, dev).start()
-        return carry
-
-    lax.fori_loop(1, devs, send_tiles, 0)
-    for k in range(caps):
-        tiles_in[dev, k] = tiles[jnp.maximum(owner[dev, k, dev], 0)]
-
-    def wait_tiles(i, carry):
-        other = lax.rem(dev + i, devs)
-        pltpu.make_async_remote_copy(
-            src_ref=tiles_out.at[other],
-            dst_ref=tiles_in.at[other],
-            send_sem=tile_sent.at[other],
-            recv_sem=tile_got.at[other],
-            device_id={"half": half, "dev": other},
-            device_id_type=MESH,
-        ).wait()
-        return carry
-
     slot_total = devs * caps
     select_shape = (slot_total, scan_count * block_total)
     slot_iota = lax.broadcasted_iota(jnp.int32, select_shape, 0)
@@ -273,17 +264,6 @@
 
     select = lax.fori_loop(
         0, scan_count * block_total, mark, jnp.zeros(select_shape, jnp.float32)
-    ).astype(jnp.bfloat16)
-    place_shape = (per_cycle, slot_total)
-    tile_iota = lax.broadcasted_iota(jnp.int32, place_shape, 0)
-    place_iota = lax.broadcasted_iota(jnp.int32, place_shape, 1)
-
-    def mark_tile(i, placing):
-        tile = owner[dev, i % caps, i // caps]
-        return jnp.where((tile_iota == tile) & (place_iota == i), 1.0, placing)
-
-    placing = lax.fori_loop(
-        0, slot_total, mark_tile, jnp.zeros(place_shape, jnp.float32)
     ).astype(jnp.bfloat16)
     lax.fori_loop(1, devs, wait_tiles, 0)
 
@@ -331,7 +311,7 @@
 
         lax.fori_loop(0, block_total // group, body, 0)
 
-    group = 16
+    group = 32
     while block_total % group:
         group //= 2
     together(lambda b: sample(0, b), group)
@@ -384,16 +364,40 @@
         back_copy(other, other).wait()
         return carry
 
+    place_shape = (per_cycle, slot_total)
+    tile_iota = lax.broadcasted_iota(jnp.int32, place_shape, 0)
+    place_iota = lax.broadcasted_iota(jnp.int32, place_shape, 1)
+
+    def mark_tile(i, placing):
+        tile = owner[dev, i % caps, i // caps]
+        return jnp.where((tile_iota == tile) & (place_iota == i), 1.0, placing)
+
+    placing = lax.fori_loop(
+        0, slot_total, mark_tile, jnp.zeros(place_shape, jnp.float32)
+    ).astype(jnp.bfloat16)
+
+    def drain_coeff(i, carry):
+        other = lax.rem(mine + i, everyone)
+        there, at = other // devs, lax.rem(other, devs)
+        coeff_copy(there, at, there, at, other, other).wait_send()
+        return carry
+
+    lax.fori_loop(1, everyone, drain_coeff, 0)
+
+    def drain_tiles(i, carry):
+        other = lax.rem(dev + i, devs)
+        tile_copy(other, other).wait_send()
+        return carry
+
+    lax.fori_loop(1, devs, drain_tiles, 0)
     lax.fori_loop(1, devs, wait_back, 0)
     for e in range(devs):
         for k in range(caps):
             sums[e * caps + k] = back_in[e, k].astype(jnp.float32)
     for f in range(fields):
-        own_tiles[:, f, :] = jnp.dot(
+        out[f // ROWS, :, f % ROWS, :] = jnp.dot(
             placing, sums[:, f, :].astype(jnp.bfloat16), preferred_element_type=jnp.float32
         )
-    for a in range(per_cycle):
-        out[0, :, a * TILE : (a + 1) * TILE] = own_tiles[a]
 
 
 def whole_part(
@@ -412,7 +416,9 @@
     loads = (orders, field_mix, alm, legendre, pix, noise)
     return pl.pallas_call(
         whole_kernel,
-        out_shape=jax.ShapeDtypeStruct((1, fields, NPHI), jnp.float32),
+        out_shape=jax.ShapeDtypeStruct(
+            (fields // ROWS, NPHI // TILE, ROWS, TILE), jnp.float32
+        ),
         in_specs=[pl.BlockSpec(memory_space=SMEM)] * 4
         + [pl.BlockSpec(memory_space=pltpu.HBM)] * len(loads),
         out_specs=pl.BlockSpec(memory_space=VMEM),
@@ -429,7 +435,6 @@
             VMEM((length // COLS * fields, COLS), jnp.bfloat16),
             VMEM((blocks, fields, TILE), jnp.float32),
             VMEM((devs * caps, fields, TILE), jnp.float32),
-            VMEM((NPHI // TILE, fields, TILE), jnp.float32),
             VMEM(exchanged, jnp.bfloat16),
             VMEM(exchanged, jnp.bfloat16),
             pltpu.SemaphoreType.DMA((len(loads),)),
@@ -464,7 +469,7 @@
     order_slots, parts, fields, ells = alm.shape
     cycles = legendre.shape[2]
     owner = fetch_list.transpose(0, 2, 1)
-    return whole_part(
+    binned = whole_part(
         owner,
         scan_tiles,
         block_tile,
@@ -478,6 +483,8 @@
         devs,
         halves,
     )
+    binned = binned.transpose(0, 2, 1, 3).reshape(1, fields, NPHI)
+    return binned * (1.0 / math.sqrt(2.0 * order_ids.shape[0]))
 
 
 def solution(mesh):

time: 39.9 us -> 43.3 us (1.085)
  Pallas kernels: 38 us -> 41.4 us
  other arithmetic: 0 us -> 1.67 us
  local copies, waits for them, and re-layouts: 1.67 us -> 0 us
    pallas_call x1, Pallas kernels: 38 us -> 41.4 us  [whole_part(): pl.pallas_call(whole_kernel, out_shape=jax.ShapeDtypeStruct((fields // RO...]
    mul x0 -> x1, other arithmetic: none -> 1.67 us  [local(): return binned * (1.0 / math.sqrt(2.0 * order_ids.shape[0]))]
    unnamed x1 -> x0, local copies, waits for them, and re-layouts: 1.67 us -> none
where the time goes in v6:
time: 43.3 us; the launch traced here: 43.1 us
  Pallas kernels  41.4 us (96%)
  other arithmetic  1.67 us (4%)
    pallas_call x1, Pallas kernels, whole_part(): pl.pallas_call(whole_kernel, out_shape=jax.ShapeDtypeStruct((fields // RO...  41.4 us
    mul x1, other arithmetic, local(): return binned * (1.0 / math.sqrt(2.0 * order_ids.shape[0]))  1.67 us

profile of v6, /device:TPU:0, one launch (start us, length us, event | category | flops | bytes accessed | tf_op | source)
XLA Modules:
  0.0 43.1 jit_solution(1393397080206960531)
XLA Ops:
  0.0 41.4 %whole.1 = f32[2,32,8,128]{3,2,1,0:T(8,128)} custom-call(s32[16,2,16]{2,1,0:T(2,128)} %bitcast.12, s32[4,32]{1,0:T(4,128)} %scan_tiles.1, s32[4,32]{1,0:T(4,128)} %block_tile.1, f32[4]{0:T(128)} %scan_weight.1, s32[1,128]{1,0:T(1,128)} %bitcast.13, f32[16,32]{1,0:T(8,128)} %mix_hbm.1, bf16[256,2048]{1,0:T(8,128)(2,1)} %bitcast.10, ...), custom_call_target="tpu_custom_call" | custom-call | tf_op jit(solution)/shard_map/whole/pallas_call | solution.py:417
  41.4 1.7 %multiply_bitcast_fusion = f32[1,16,4096]{2,1,0:T(8,128)} fusion(f32[2,32,8,128]{3,2,1,0:T(8,128)} %whole.1), kind=kLoop, calls=%fused_computation | loop fusion | flops 65536 | bytes 524288 | tf_op jit(solution)/shard_map/mul | solution.py:487

commit v7 on v5

--- a/solution.py
+++ b/solution.py
@@ -149,11 +149,8 @@
 
     def wait_coeff(i, carry):
         other = lax.rem(mine + i, everyone)
-        copy = coeff_copy(
-            other // devs, lax.rem(other, devs), other // devs, lax.rem(other, devs), other, other
-        )
-        copy.wait_recv()
-        copy.wait_send()
+        there, at = other // devs, lax.rem(other, devs)
+        coeff_copy(there, at, there, at, other, other).wait_recv()
         return carry
 
     scan_count, block_total = block_tile.shape
@@ -251,14 +248,7 @@
 
     def wait_tiles(i, carry):
         other = lax.rem(dev + i, devs)
-        pltpu.make_async_remote_copy(
-            src_ref=tiles_out.at[other],
-            dst_ref=tiles_in.at[other],
-            send_sem=tile_sent.at[other],
-            recv_sem=tile_got.at[other],
-            device_id={"half": half, "dev": other},
-            device_id_type=MESH,
-        ).wait()
+        tile_copy(other, other).wait_recv()
         return carry
 
     slot_total = devs * caps
@@ -272,18 +262,7 @@
         return jnp.where((slot_iota == slot) & (block_iota == i), 1.0, select)
 
     select = lax.fori_loop(
-        0, scan_count * block_total, mark, jnp.zeros(select_shape, jnp.float32)
-    ).astype(jnp.bfloat16)
-    place_shape = (per_cycle, slot_total)
-    tile_iota = lax.broadcasted_iota(jnp.int32, place_shape, 0)
-    place_iota = lax.broadcasted_iota(jnp.int32, place_shape, 1)
-
-    def mark_tile(i, placing):
-        tile = owner[dev, i % caps, i // caps]
-        return jnp.where((tile_iota == tile) & (place_iota == i), 1.0, placing)
-
-    placing = lax.fori_loop(
-        0, slot_total, mark_tile, jnp.zeros(place_shape, jnp.float32)
+        0, scan_count * block_total, mark, jnp.zeros(select_shape, jnp.float32), unroll=8
     ).astype(jnp.bfloat16)
     lax.fori_loop(1, devs, wait_tiles, 0)
 
@@ -384,6 +363,32 @@
         back_copy(other, other).wait()
         return carry
 
+    place_shape = (per_cycle, slot_total)
+    tile_iota = lax.broadcasted_iota(jnp.int32, place_shape, 0)
+    place_iota = lax.broadcasted_iota(jnp.int32, place_shape, 1)
+
+    def mark_tile(i, placing):
+        tile = owner[dev, i % caps, i // caps]
+        return jnp.where((tile_iota == tile) & (place_iota == i), 1.0, placing)
+
+    placing = lax.fori_loop(
+        0, slot_total, mark_tile, jnp.zeros(place_shape, jnp.float32), unroll=8
+    ).astype(jnp.bfloat16)
+
+    def drain_coeff(i, carry):
+        other = lax.rem(mine + i, everyone)
+        there, at = other // devs, lax.rem(other, devs)
+        coeff_copy(there, at, there, at, other, other).wait_send()
+        return carry
+
+    lax.fori_loop(1, everyone, drain_coeff, 0)
+
+    def drain_tiles(i, carry):
+        other = lax.rem(dev + i, devs)
+        tile_copy(other, other).wait_send()
+        return carry
+
+    lax.fori_loop(1, devs, drain_tiles, 0)
     lax.fori_loop(1, devs, wait_back, 0)
     for e in range(devs):
         for k in range(caps):

time: 39.9 us -> 39.8 us (level)
  no operation moved by 1% of the time
where the time goes in v7:
time: 39.8 us; the launch traced here: 39.5 us
  Pallas kernels  37.9 us (95%)
  local copies, waits for them, and re-layouts  1.67 us (4%)
    pallas_call x1, Pallas kernels, whole_part(): pl.pallas_call(whole_kernel, out_shape=jax.ShapeDtypeStruct((1, fields, N...  37.9 us
    unnamed x1, local copies, waits for them, and re-layouts  1.67 us

profile of v7, /device:TPU:0, one launch (start us, length us, event | category | flops | bytes accessed | tf_op | source)
XLA Modules:
  0.0 39.5 jit_solution(14665694320603162702)
XLA Ops:
  0.0 37.9 %whole.1 = f32[1,16,4096]{2,1,0:T(8,128)} custom-call(s32[16,2,16]{2,1,0:T(2,128)} %bitcast.8, s32[4,32]{1,0:T(4,128)} %scan_tiles.1, s32[4,32]{1,0:T(4,128)} %block_tile.1, f32[4]{0:T(128)} %scan_weight.1, s32[1,128]{1,0:T(1,128)} %bitcast.9, f32[16,32]{1,0:T(8,128)} %mix_hbm.1, bf16[256,2048]{1,0:T(8,128)(2,1)} %bitcast.6, bf16[128,2048]{1,0:T(8,128)(2,1)} %bitcast.7, ...), custom_call_target="tpu_custom_call" | custom-call | tf_op jit(solution)/shard_map/whole/pallas_call | solution.py:418
  37.9 1.7 %copy.12 = f32[1,16,4096]{2,1,0:T(8,128)} copy(f32[1,16,4096]{2,1,0:T(8,128)} %whole.1) | data formatting | bytes 524288
